TPU v7x, 512 devices: a whole 4x8x8 slice. The times are simulated.
512 devices in a mesh: dp: 16 (over z, core), shard: 32 (over x, y).
Axes of the slice: x: 4, y: 8, z: 8, core: 2. Of those that a mesh axis runs over, the one named last changes fastest.
Arguments:
- table: bfloat16 [32768, 160], P('shard'), may hold values from -6 to 6
- slot_rows: int32 [16, 32, 32, 32], P('dp', 'shard'), may hold values from 0 to 1023
- slot_counts: int32 [16, 32, 32], P('dp', 'shard'), may hold values from 8 to 32, as said below
- positions: int32 [8192, 128], P(('dp', 'shard')), may hold values from 0 to 1023
- fm_proj: bfloat16 [128, 8], replicated, may hold values from -0.5 to 0.5
- ln_gain: float32 [1024], replicated, may hold values from 0.1 to 1.9
- w_up: bfloat16 [1024, 4096], P(None, 'shard'), may hold values from -0.1875 to 0.1875
- w_down: bfloat16 [4096, 2560], P('shard'), may hold values from -0.09375 to 0.09375
- w_lcb: bfloat16 [112, 128], replicated, may hold values from -0.5 to 0.5
- cotangent: bfloat16 [8192, 128, 160], P(('dp', 'shard')), may hold values from -6 to 6
Outputs:
- mixed: bfloat16 [8192, 128, 160], P(('dp', 'shard'))
- grad_table: float32 [32768, 160], P('shard')
- grad_w_up: bfloat16 [1024, 4096], P('dp', 'shard')
- grad_w_down: bfloat16 [4096, 2560], P('shard', 'dp')
- grad_fm_proj: float32 [128, 8], replicated
- grad_w_lcb: float32 [112, 128], replicated
- grad_ln_gain: float32 [1024], replicated
Inputs may be any that keep to these rules, and one draw needn't show every extreme that they name: `slot_counts`: every device has some owner to which all 32 of its slots are live.
All inputs are finite; a program needn't handle non-finite values.
Results may differ from a plain program's by a relative error of at most 0.018.
Values may be sent and summed in bfloat16 or wider, within the bound.
No kernel may reach another device: no remote copies, remote signals or barrier semaphores. Data moves between devices by JAX's collectives and lax.ppermute only.
A program may use at most 64 MiB of HBM per device.

v0:
```python
import jax
import jax.numpy as jnp
from jax import lax
from jax.sharding import PartitionSpec as P

F = 128
K = 8
NF = 16
CAP = 32


def layer_norm(flat):
    center = flat - jnp.mean(flat, axis=1, keepdims=True)
    inverse_std = lax.rsqrt(jnp.mean(center * center, axis=1, keepdims=True) + 1e-05)
    return (center * inverse_std, inverse_std)


def body(
    table, slot_rows, slot_counts, positions, fm_proj, ln_gain, w_up, w_down, w_lcb, cotangent
):
    highest = lax.Precision.HIGHEST
    members = lax.axis_size("shard")
    batch = positions.shape[0]
    width = table.shape[1]
    rows_here = table.shape[0]
    request = slot_rows.reshape(members, CAP)
    counts_here = slot_counts.reshape(members)
    live_mask = lax.broadcasted_iota(jnp.int32, (members, CAP), 1) < counts_here[:, None]
    asked = lax.all_to_all(request, "shard", split_axis=0, concat_axis=0, tiled=True)
    fetched = lax.all_to_all(table[asked], "shard", split_axis=0, concat_axis=0, tiled=True)
    fetched = jnp.where(live_mask[:, :, None], fetched, jnp.zeros((), fetched.dtype))
    embeds = fetched.reshape(members * CAP, width)[positions]
    embeds_f = embeds.astype(jnp.float32)
    projector = fm_proj.astype(jnp.float32)
    compressed = jnp.einsum("bfd,fk->bdk", embeds_f, projector, precision=highest)
    gram = jnp.einsum("bfd,bdk->bfk", embeds_f, compressed, precision=highest).reshape(batch, F * K)
    normal_part, inverse_std = layer_norm(gram)
    normed = (normal_part * ln_gain).astype(jnp.bfloat16)
    group_normed = lax.all_gather(normed, "shard", axis=0, tiled=True)
    preact = jnp.dot(group_normed, w_up, preferred_element_type=jnp.float32)
    activ = jax.nn.silu(preact).astype(jnp.bfloat16)
    rows_taken = activ
    mlp_out = lax.psum_scatter(
        jnp.dot(rows_taken, w_down, preferred_element_type=jnp.float32).astype(jnp.bfloat16),
        "shard",
        scatter_dimension=0,
        tiled=True,
    ).astype(jnp.float32)
    linear_part = jnp.einsum("lf,bfd->bld", w_lcb, embeds, preferred_element_type=jnp.float32)
    joined = jnp.concatenate([mlp_out.reshape(batch, NF, width), linear_part], axis=1)
    mixed = (embeds_f + joined).astype(jnp.bfloat16)
    grad_mlp = cotangent[:, :NF, :].reshape(batch, NF * width)
    group_grads = lax.all_gather(grad_mlp, "shard", axis=0, tiled=True)
    down_part = lax.dot_general(
        activ, group_grads, (((0,), (0,)), ((), ())), preferred_element_type=jnp.float32
    )
    d_hidden = lax.dot_general(
        group_grads, w_down, (((1,), (1,)), ((), ())), preferred_element_type=jnp.float32
    )
    sigmoid_pre = jax.nn.sigmoid(preact)
    d_pre = (d_hidden * sigmoid_pre * (1.0 + preact * (1.0 - sigmoid_pre))).astype(jnp.bfloat16)
    up_part = lax.dot_general(
        group_normed, d_pre, (((0,), (0,)), ((), ())), preferred_element_type=jnp.float32
    )
    rows_taken = d_pre
    d_normed = lax.psum_scatter(
        lax.dot_general(
            rows_taken, w_up, (((1,), (1,)), ((), ())), preferred_element_type=jnp.float32
        ).astype(jnp.bfloat16),
        "shard",
        scatter_dimension=0,
        tiled=True,
    ).astype(jnp.float32)
    down_summed, up_summed = (
        lax.psum_scatter(
            down_part.astype(jnp.bfloat16), "dp", scatter_dimension=1, tiled=True
        ).astype(jnp.float32),
        lax.psum_scatter(
            up_part.astype(jnp.bfloat16), "dp", scatter_dimension=0, tiled=True
        ).astype(jnp.float32),
    )
    grad_w_down = down_summed.astype(jnp.bfloat16)
    grad_w_up = up_summed.astype(jnp.bfloat16)
    gain_part = jnp.sum(d_normed * normal_part, axis=0)
    scaled = d_normed * ln_gain
    d_gram = inverse_std * (
        scaled
        - jnp.mean(scaled, axis=1, keepdims=True)
        - normal_part * jnp.mean(scaled * normal_part, axis=1, keepdims=True)
    )
    d_gram = d_gram.reshape(batch, F, K)
    d_compressed = jnp.einsum("bfd,bfk->bdk", embeds_f, d_gram, precision=highest)
    proj_part = jnp.einsum("bfd,bdk->fk", embeds_f, d_compressed, precision=highest)
    grad_linear = cotangent[:, NF:, :]
    lcb_part = jnp.einsum("bld,bfd->lf", grad_linear, embeds, preferred_element_type=jnp.float32)
    d_embeds = cotangent.astype(jnp.float32)
    d_embeds = d_embeds + jnp.einsum("bfk,bdk->bfd", d_gram, compressed, precision=highest)
    d_embeds = d_embeds + jnp.einsum("fk,bdk->bfd", projector, d_compressed, precision=highest)
    d_embeds = d_embeds + jnp.einsum(
        "lf,bld->bfd", w_lcb, grad_linear, preferred_element_type=jnp.float32
    )
    slot_grad = jax.ops.segment_sum(
        d_embeds.reshape(-1, width), positions.reshape(-1), num_segments=members * CAP
    ).reshape(members, CAP, width)
    slot_grad = jnp.where(live_mask[:, :, None], slot_grad, jnp.zeros((), slot_grad.dtype))
    returned = lax.all_to_all(
        slot_grad.astype(jnp.bfloat16), "shard", split_axis=0, concat_axis=0, tiled=True
    ).astype(slot_grad.dtype)
    table_part = jax.ops.segment_sum(
        returned.reshape(-1, width), asked.reshape(-1), num_segments=rows_here
    )
    grad_ln_gain, grad_fm_proj, grad_w_lcb = lax.psum(
        (gain_part, proj_part, lcb_part), ("dp", "shard")
    )
    grad_table = lax.psum(table_part.astype(jnp.bfloat16), "dp").astype(jnp.float32)
    return (mixed, grad_table, grad_w_up, grad_w_down, grad_fm_proj, grad_w_lcb, grad_ln_gain)


def solution(mesh):
    placed = (
        P("shard", None),
        P("dp", "shard", None, None),
        P("dp", "shard", None),
        P(("dp", "shard"), None),
        P(),
        P(),
        P(None, "shard"),
        P("shard", None),
        P(),
        P(("dp", "shard"), None, None),
    )
    return jax.shard_map(
        body,
        mesh=mesh,
        in_specs=placed,
        out_specs=(
            P(("dp", "shard"), None, None),
            P("shard", None),
            P("dp", "shard"),
            P("shard", "dp"),
            P(),
            P(),
            P(),
        ),
        check_vma=False,
    )
```

profile of v0, /device:TPU:1, one launch (start us, length us, event | category | flops | bytes accessed | tf_op | source)
XLA Modules:
  0.0 1206.3 jit_solution(16223731058998832824)
XLA Ops:
  7.2 10.6 all-to-all-start
  19.0 7.4 all-to-all-done
  26.5 5.0 gather_fusion
  31.5 3.9 all-to-all-start.1
  35.5 12.8 %all-to-all-done.1 = bf16[32,32,160]{2,1,0:T(8,128)(2,1)S(1)} async-done(((bf16[32,32,160]{2,1,0:T(8,128)(2,1)}), bf16[32,32,160]{2,1,0:T(8,128)(2,1)S(1)}, u32[]{:S(2)}, u32[]{:S(2)}) %all-to-all-start.1) | async-done | bytes 327712 | tf_op jit(solution)/shard_map/all_to_all | solution.py:30
  48.6 7.5 gather_fusion.1
  67.3 80.4 %all-gather.3.cloned.1.call-done = bf16[512,1024]{1,0:T(8,128)(2,1)} async-done(((bf16[16,1024]{1,0:T(8,128)(2,1)}), bf16[512,1024]{1,0:T(8,128)(2,1)}) %all-gather.3.cloned.1.call-update) | async-done | bytes 1048592 | tf_op jit(solution)/shard_map/all_gather | solution.py:39
  149.4 85.2 %all-gather.5.cloned.1.call-done = bf16[512,2560]{1,0:T(8,128)(2,1)} async-done(((bf16[16,2560]{1,0:T(8,128)(2,1)}), bf16[512,2560]{1,0:T(8,128)(2,1)}) %all-gather.5.cloned.1.call-update) | async-done | bytes 2621456 | tf_op jit(solution)/shard_map/all_gather | solution.py:53
  234.6 2.6 fusion.4
  239.4 2.3 convolution_convert_fusion
  244.0 210.9 %reduce-scatter.7.cloned.1.call-done = bf16[16,1024]{1,0:T(8,128)(2,1)} async-done(((bf16[512,1024]{1,0:T(8,128)(2,1)}), bf16[16,1024]{1,0:T(8,128)(2,1)}) %reduce-scatter.7.cloned.1.call-update) | async-done | bytes 32784 | tf_op jit(solution)/shard_map/reduce_scatter | solution.py:66
  461.3 3.5 fusion.1
  464.8 2.8 copy.67
  467.6 13.0 %scatter_custom_fusion = f32[1024,160]{1,0:T(8,128)} fusion(s32[2048]{0:T(1024)} %bitcast.77, f32[2048,160]{1,0:T(8,128)} %bitcast.74, f32[]{:T(128)} %constant.10.clone.1), kind=kCustom, calls=%fused_computation.26 | custom fusion | flops 327680 | bytes 655872 | tf_op jit(solution)/shard_map/scatter-add | solution.py:102
  482.8 6.8 all-to-all-start.2
  490.9 12.0 all-to-all-done.2
  502.9 7.0 scatter_custom_fusion.1
  512.1 2.4 convolution_convert_fusion.3
  514.8 3.8 convolution_convert_fusion.1
  525.1 158.3 %reduce-scatter.5.cloned.1.call-done = bf16[16,2560]{1,0:T(8,128)(2,1)} async-done(((bf16[512,2560]{1,0:T(8,128)(2,1)}), bf16[16,2560]{1,0:T(8,128)(2,1)}) %reduce-scatter.5.cloned.1.call-update) | async-done | bytes 81936 | tf_op jit(solution)/shard_map/reduce_scatter | solution.py:43
  687.3 117.9 %all-reduce.4.cloned.1.call-done = bf16[1024,160]{1,0:T(8,128)(2,1)} async-done(((bf16[1024,160]{1,0:T(8,128)(2,1)}), bf16[1024,160]{1,0:T(8,128)(2,1)}) %all-reduce.4.cloned.1.call-update) | async-done | bytes 327696 | tf_op jit(solution)/shard_map/psum | solution.py:115
  807.2 57.9 %reduce-scatter.9.cloned.1.call-done = bf16[64,128]{1,0:T(8,128)(2,1)} async-done(((bf16[1024,128]{1,0:T(8,128)(2,1)}), bf16[64,128]{1,0:T(8,128)(2,1)}) %reduce-scatter.9.cloned.1.call-update) | async-done | bytes 16400 | tf_op jit(solution)/shard_map/reduce_scatter | solution.py:78
  865.1 61.2 %reduce-scatter.11.cloned.1.call-done = bf16[128,160]{0,1:T(8,128)(2,1)} async-done(((bf16[128,2560]{0,1:T(8,128)(2,1)}), bf16[128,160]{0,1:T(8,128)(2,1)}) %reduce-scatter.11.cloned.1.call-update) | async-done | bytes 40976 | tf_op jit(solution)/shard_map/reduce_scatter | solution.py:75
  926.3 269.1 %all-reduce.6.cloned.1.call-done = (f32[128,8]{0,1:T(8,128)}, f32[112,128]{1,0:T(8,128)}, f32[1024]{0:T(1024)}) async-done(((f32[128,8]{0,1:T(8,128)}, f32[112,128]{1,0:T(8,128)}, f32[1024]{0:T(1024)}), (f32[128,8]{0,1:T(8,128)}, f32[112,128]{1,0:T(8,128)}, f32[1024]{0:T(1024)})) %all-reduce.6.cloned.1.call-update) | async-done | bytes 65552 | tf_op jit(solution)/shard_map/psum | solution.py:112
  (107 shorter events, 47.6 us)
Async XLA Ops:
  7.2 227.4 %copy-start = (bf16[128,2560]{1,0:T(8,128)(2,1)S(1)}, bf16[128,2560]{1,0:T(8,128)(2,1)}, u32[]{:S(2)}) copy-start(bf16[128,2560]{1,0:T(8,128)(2,1)} %param.17) | copy-start | bytes 1966084
  7.2 19.2 %all-to-all-start = ((s32[32,1,32]{2,1,0:T(1,128)}), s32[32,1,32]{2,1,0:T(1,128)S(1)}, u32[]{:S(2)}, u32[]{:S(2)}) async-start(s32[32,1,32]{2,1,0:T(1,128)} %bitcast.76), calls=%async_computation | async-start | bytes 32768 | tf_op jit(solution)/shard_map/all_to_all | solution.py:29
  26.5 8.9 copy-start.21
  26.5 9.0 copy-start.19
  31.5 16.9 %all-to-all-start.1 = ((bf16[32,32,160]{2,1,0:T(8,128)(2,1)}), bf16[32,32,160]{2,1,0:T(8,128)(2,1)S(1)}, u32[]{:S(2)}, u32[]{:S(2)}) async-start(bf16[32,32,160]{2,1,0:T(8,128)(2,1)} %bitcast.3), calls=%async_computation.1 | async-start | bytes 1048576 | tf_op jit(solution)/shard_map/all_to_all | solution.py:30
  35.4 112.3 %all-gather.3.cloned.1.call-start = ((), (), s32[]{:S(2)}) async-start(), calls=%async_computation.7 | async-start | bytes 1081344 | tf_op jit(solution)/shard_map/all_gather | solution.py:39
  35.5 13.0 %copy-start.13 = (pred[32,32]{1,0:T(8,128)(4,1)}, pred[32,32]{1,0:T(8,128)(4,1)S(1)}, u32[]{:S(2)}) copy-start(pred[32,32]{1,0:T(8,128)(4,1)S(1)} %iota_compare_fusion) | copy-start | bytes 3076
  58.8 7.3 copy-start.1
  64.4 83.3 %copy-start.7 = (bf16[1024,128]{1,0:T(8,128)(2,1)S(1)}, bf16[1024,128]{1,0:T(8,128)(2,1)}, u32[]{:S(2)}) copy-start(bf16[1024,128]{1,0:T(8,128)(2,1)} %param.16) | copy-start | bytes 786436
  66.0 168.5 %all-gather.5.cloned.1.call-start = ((), (), s32[]{:S(2)}) async-start(), calls=%async_computation.9 | async-start | bytes 2703360 | tf_op jit(solution)/shard_map/all_gather | solution.py:53
  67.3 387.7 %reduce-scatter.7.cloned.1.call-start = ((), (), s32[]{:S(2)}) async-start(), calls=%async_computation.10 | async-start | bytes 1081344 | tf_op jit(solution)/shard_map/reduce_scatter | solution.py:66
  239.2 444.2 %reduce-scatter.5.cloned.1.call-start = ((), (), s32[]{:S(2)}) async-start(), calls=%async_computation.8 | async-start | bytes 2703360 | tf_op jit(solution)/shard_map/reduce_scatter | solution.py:43
  242.5 212.4 %copy-start.6 = (f32[16,1024]{1,0:T(8,128)S(1)}, f32[16,1024]{1,0:T(8,128)}, u32[]{:S(2)}) copy-start(f32[16,1024]{1,0:T(8,128)} %copy.48) | copy-start | bytes 196612
  242.5 212.4 %copy-start.15 = (f32[1024]{0:T(1024)S(1)}, f32[1024]{0:T(1024)}, u32[]{:S(2)}) copy-start(f32[1024]{0:T(1024)} %param.15) | copy-start | bytes 12292
  242.5 212.4 %copy-start.18 = (f32[16]{0:T(128)S(1)}, f32[16]{0:T(128)}, u32[]{:S(2)}) copy-start(f32[16]{0:T(128)} %broadcast_multiply_fusion.2) | copy-start | bytes 196
  242.5 212.4 %copy-start.20 = (f32[16]{0:T(128)S(1)}, f32[16]{0:T(128)}, u32[]{:S(2)}) copy-start(f32[16]{0:T(128)} %add_rsqrt_fusion) | copy-start | bytes 196
  456.4 3.6 copy-start.17
  464.8 15.8 %copy-start.14 = (pred[32,32]{1,0:T(8,128)(4,1)S(1)}, pred[32,32]{1,0:T(8,128)(4,1)}, u32[]{:S(2)}) copy-start(pred[32,32]{1,0:T(8,128)(4,1)} %copy-done.13) | copy-start | bytes 3076
  482.8 20.1 %all-to-all-start.2 = ((bf16[32,32,160]{2,1,0:T(8,128)(2,1)}), bf16[32,32,160]{2,1,0:T(8,128)(2,1)}, u32[]{:S(2)}, u32[]{:S(2)}) async-start(bf16[32,32,160]{2,1,0:T(8,128)(2,1)} %select_convert_fusion), calls=%async_computation.4 | async-start | bytes 1048576 | tf_op jit(solution)/shard_map/all_to_all | solution.py:106
  489.6 315.6 %all-reduce.4.cloned.1.call-start = ((), (), s32[]{:S(2)}) async-start(), calls=%async_computation.11 | async-start | bytes 1048576 | tf_op jit(solution)/shard_map/psum | solution.py:115
  512.0 353.0 %reduce-scatter.9.cloned.1.call-start = ((), (), s32[]{:S(2)}) async-start(), calls=%async_computation.12 | async-start | bytes 278528 | tf_op jit(solution)/shard_map/reduce_scatter | solution.py:78
  514.5 411.8 %reduce-scatter.11.cloned.1.call-start = ((), (), s32[]{:S(2)}) async-start(), calls=%async_computation.13 | async-start | bytes 696320 | tf_op jit(solution)/shard_map/reduce_scatter | solution.py:75
  518.6 676.9 %all-reduce.6.cloned.1.call-start = ((), (), s32[]{:S(2)}) async-start(), calls=%async_computation.14 | async-start | bytes 131072 | tf_op jit(solution)/shard_map/psum | solution.py:112
  525.1 159.8 %copy-start.3 = (f32[16,112,160]{1,2,0:T(8,128)S(1)}, f32[16,112,160]{1,2,0:T(8,128)}, u32[]{:S(2)}) copy-start(f32[16,112,160]{1,2,0:T(8,128)} %convolution_bitcast_fusion.2) | copy-start | bytes 3440644
  (9 other events, 13.6 us)
Sparse Core Ops, SparseCore 0:
  66.2 81.4 all-gather.2
  151.4 83.0 all-gather.4
  239.3 215.5 reduce-scatter.6
  459.2 224.1 reduce-scatter.4
  685.6 119.5 all-reduce.3
  808.6 56.4 reduce-scatter.8
  868.4 57.8 reduce-scatter.10
  933.4 262.0 all-reduce.5
where the time goes:
time: 1210 us
  waiting for transfers between devices  1070 us (88%)
  local copies, waits for them, and re-layouts  35 us (3%)
  other arithmetic  33.7 us (3%)
  matrix products  27.9 us (2%)
  starting transfers between devices  22 us (2%)
  between operations  14.4 us (1%)
    psum x1, waiting for transfers between devices, body(): lax.psum((gain_part, proj_part, lcb_part), ('dp', 'shard'))  269 us
    reduce_scatter x1, waiting for transfers between devices, body(): lax.psum_scatter(lax.dot_general(rows_taken, w_up, (((1,), (1,)), ((), ()...  211 us
    reduce_scatter x1, waiting for transfers between devices, body(): lax.psum_scatter(jnp.dot(rows_taken, w_down, preferred_element_type=jnp.f...  158 us
    psum x1, waiting for transfers between devices, body(): lax.psum(table_part.astype(jnp.bfloat16), 'dp').astype(jnp.float32)  118 us
    all_gather x1, waiting for transfers between devices, body(): group_grads = lax.all_gather(grad_mlp, 'shard', axis=0, tiled=True)  85.2 us
    all_gather x1, waiting for transfers between devices, body(): group_normed = lax.all_gather(normed, 'shard', axis=0, tiled=True)  80.4 us
    reduce_scatter x1, waiting for transfers between devices, body(): lax.psum_scatter(down_part.astype(jnp.bfloat16), 'dp', scatter_dimension=...  61.2 us
    reduce_scatter x1, waiting for transfers between devices, body(): lax.psum_scatter(up_part.astype(jnp.bfloat16), 'dp', scatter_dimension=0,...  57.9 us
  transfers between devices with their start and end apart: 11, of which 11 were waited for; matrix products, arithmetic and copies ran while one was open for 5% of the time, Pallas kernels for 0%

commit v1 on v0

v1 whole, which is shorter than its diff:
```python
import jax
import jax.numpy as jnp
from jax import lax
from jax.sharding import PartitionSpec as P

F = 128
K = 8
NF = 16
CAP = 32
LANES = 128


def layer_norm(flat):
    center = flat - jnp.mean(flat, axis=1, keepdims=True)
    inverse_std = lax.rsqrt(jnp.mean(center * center, axis=1, keepdims=True) + 1e-05)
    return (center * inverse_std, inverse_std)


def exchange(blocks, axis):
    return lax.all_to_all(blocks, axis, split_axis=0, concat_axis=0, tiled=True)


def spread(block, axis):
    count = lax.axis_size(axis)
    return exchange(jnp.broadcast_to(block[None], (count, *block.shape)), axis)


def summed(blocks, axis):
    return jnp.sum(exchange(blocks, axis).astype(jnp.float32), axis=0)


def body(
    table, slot_rows, slot_counts, positions, fm_proj, ln_gain, w_up, w_down, w_lcb, cotangent
):
    highest = lax.Precision.HIGHEST
    f32, bf16 = jnp.float32, jnp.bfloat16
    members = lax.axis_size("shard")
    groups = lax.axis_size("dp")
    batch = positions.shape[0]
    width = table.shape[1]
    rows_here = table.shape[0]
    slots = members * CAP
    hidden = w_up.shape[1]
    request = slot_rows.reshape(members, CAP)
    counts_here = slot_counts.reshape(members)

    grad_mlp = cotangent[:, :NF, :].reshape(batch, NF * width)
    group_grads = lax.all_gather(grad_mlp, "shard", axis=0, tiled=True)

    asked = exchange(request, "shard").reshape(slots)
    row_ids = lax.broadcasted_iota(jnp.int32, (slots, rows_here), 1)
    asked_hot = (asked[:, None] == row_ids).astype(bf16)
    sent = jnp.dot(asked_hot, table, preferred_element_type=f32).astype(bf16)
    fetched = exchange(sent.reshape(members, CAP, width), "shard")
    live_mask = lax.broadcasted_iota(jnp.int32, (members, CAP), 1) < counts_here[:, None]
    fetched = jnp.where(live_mask[:, :, None], fetched, jnp.zeros((), bf16)).reshape(slots, width)
    flat_positions = positions.reshape(batch * F)
    slot_ids = lax.broadcasted_iota(jnp.int32, (batch * F, slots), 1)
    slot_hot = (flat_positions[:, None] == slot_ids).astype(bf16)
    embeds = jnp.dot(slot_hot, fetched, preferred_element_type=f32).astype(bf16)
    embeds = embeds.reshape(batch, F, width)

    embeds_f = embeds.astype(f32)
    projector = fm_proj.astype(f32)
    compressed = jnp.einsum("bfd,fk->bdk", embeds_f, projector, precision=highest)
    gram = jnp.einsum("bfd,bdk->bfk", embeds_f, compressed, precision=highest).reshape(batch, F * K)
    normal_part, inverse_std = layer_norm(gram)
    normed = (normal_part * ln_gain).astype(bf16)
    group_normed = spread(normed, "shard").reshape(members * batch, F * K)

    preact = jnp.dot(group_normed, w_up, preferred_element_type=f32)
    d_hidden = lax.dot_general(
        group_grads, w_down, (((1,), (1,)), ((), ())), preferred_element_type=f32
    )
    sigmoid_pre = jax.nn.sigmoid(preact)
    d_pre = (d_hidden * sigmoid_pre * (1.0 + preact * (1.0 - sigmoid_pre))).astype(bf16)
    d_normed_part = lax.dot_general(
        d_pre, w_up, (((1,), (1,)), ((), ())), preferred_element_type=f32
    ).astype(bf16)
    d_normed = summed(d_normed_part.reshape(members, batch, F * K), "shard")

    activ = jax.nn.silu(preact).astype(bf16)
    mlp_part = jnp.dot(activ, w_down, preferred_element_type=f32).astype(bf16)
    mlp_out = summed(mlp_part.reshape(members, batch, NF * width), "shard")
    down_part = lax.dot_general(
        group_grads, activ, (((0,), (0,)), ((), ())), preferred_element_type=f32
    ).astype(bf16)
    up_part = lax.dot_general(
        group_normed, d_pre, (((0,), (0,)), ((), ())), preferred_element_type=f32
    ).astype(bf16)
    down_sum = summed(down_part.reshape(groups, NF * width // groups, hidden), "dp")
    grad_w_down = down_sum.astype(bf16).T
    grad_w_up = summed(up_part.reshape(groups, F * K // groups, hidden), "dp").astype(bf16)

    grad_linear = cotangent[:, NF:, :]
    linear_part = jnp.einsum("lf,bfd->bld", w_lcb, embeds, preferred_element_type=f32)
    lcb_part = jnp.einsum("bld,bfd->lf", grad_linear, embeds, preferred_element_type=f32)
    d_linear = jnp.einsum("lf,bld->bfd", w_lcb, grad_linear, preferred_element_type=f32)

    gain_part = jnp.sum(d_normed * normal_part, axis=0)
    scaled = d_normed * ln_gain
    d_gram = inverse_std * (
        scaled
        - jnp.mean(scaled, axis=1, keepdims=True)
        - normal_part * jnp.mean(scaled * normal_part, axis=1, keepdims=True)
    )
    d_gram = d_gram.reshape(batch, F, K)
    d_compressed = jnp.einsum("bfd,bfk->bdk", embeds_f, d_gram, precision=highest)
    d_embeds = cotangent.astype(f32) + d_linear
    d_embeds = d_embeds + jnp.einsum("bfk,bdk->bfd", d_gram, compressed, precision=highest)
    d_embeds = d_embeds + jnp.einsum("fk,bdk->bfd", projector, d_compressed, precision=highest)
    d_embeds = d_embeds.astype(bf16).reshape(batch * F, width)
    slot_rows_hot = (
        lax.broadcasted_iota(jnp.int32, (slots, batch * F), 0) == flat_positions[None, :]
    ).astype(bf16)
    slot_grad = jnp.dot(slot_rows_hot, d_embeds, preferred_element_type=f32)
    slot_grad = slot_grad.reshape(members, CAP, width)
    slot_grad = jnp.where(live_mask[:, :, None], slot_grad, 0.0).astype(bf16)
    returned = exchange(slot_grad, "shard").reshape(slots, width)
    row_hot = (
        lax.broadcasted_iota(jnp.int32, (rows_here, slots), 0) == asked[None, :]
    ).astype(bf16)
    table_part = lax.dot_general(
        returned, row_hot, (((0,), (1,)), ((), ())), preferred_element_type=f32
    ).astype(bf16)
    columns = rows_here // LANES
    table_part = table_part.reshape(width, columns, LANES).transpose(1, 0, 2)
    table_sum = summed(table_part.reshape(groups, -1, LANES), "dp").astype(bf16)
    table_all = spread(table_sum, "dp").reshape(columns, width, LANES)
    grad_table = table_all.transpose(0, 2, 1).reshape(rows_here, width).astype(f32)

    proj_part = jnp.einsum("bfd,bdk->fk", embeds_f, d_compressed, precision=highest)
    small = jnp.concatenate([gain_part, proj_part.reshape(-1), lcb_part.reshape(-1)])
    small = small.reshape(members, -1, LANES)
    small = summed(small, "shard")
    small = jnp.sum(spread(small, "dp"), axis=0)
    small = spread(small, "shard").reshape(-1)
    grad_ln_gain = small[: F * K]
    grad_fm_proj = small[F * K : 2 * F * K].reshape(F, K)
    grad_w_lcb = small[2 * F * K :].reshape(F - NF, F)

    joined = jnp.concatenate([mlp_out.reshape(batch, NF, width), linear_part], axis=1)
    mixed = (embeds_f + joined).astype(bf16)
    return (mixed, grad_table, grad_w_up, grad_w_down, grad_fm_proj, grad_w_lcb, grad_ln_gain)


def solution(mesh):
    placed = (
        P("shard", None),
        P("dp", "shard", None, None),
        P("dp", "shard", None),
        P(("dp", "shard"), None),
        P(),
        P(),
        P(None, "shard"),
        P("shard", None),
        P(),
        P(("dp", "shard"), None, None),
    )
    return jax.shard_map(
        body,
        mesh=mesh,
        in_specs=placed,
        out_specs=(
            P(("dp", "shard"), None, None),
            P("shard", None),
            P("dp", "shard"),
            P("shard", "dp"),
            P(),
            P(),
            P(),
        ),
        check_vma=False,
    )
```

time: 1210 us -> 377 us (0.31)
  waiting for transfers between devices: 1070 us -> 169 us
  blocking collectives: 0 us -> 53.2 us
  starting transfers between devices: 22 us -> 69.4 us
  other arithmetic: 33.7 us -> 12.8 us
  local copies, waits for them, and re-layouts: 35 us -> 19.7 us
    reduce_scatter x4 -> x0, waiting for transfers between devices: 488 us -> none  [the longest x1 211 us: body(): lax.psum_scatter(lax.dot_general(rows_taken, w_up, (((1,), (1,)), ((), ()...]
    psum x2 -> x0, waiting for transfers between devices: 387 us -> none  [the longest x1 269 us: body(): lax.psum((gain_part, proj_part, lcb_part), ('dp', 'shard'))]
    all_to_all x3 -> x11, waiting for transfers between devices: 32.2 us -> 155 us  [exchange(): return lax.all_to_all(blocks, axis, split_axis=0, concat_axis=0, tiled=True)]
    all_gather x1 -> x0, waiting for transfers between devices: 80.4 us -> none  [body(): group_normed = lax.all_gather(normed, 'shard', axis=0, tiled=True)]
    all_gather x1, waiting for transfers between devices: 85.2 us -> 14.6 us  [body(): group_grads = lax.all_gather(grad_mlp, 'shard', axis=0, tiled=True)]
    all_to_all x0 -> x2, blocking collectives: none -> 53.2 us  [exchange(): return lax.all_to_all(blocks, axis, split_axis=0, concat_axis=0, tiled=True)]
    all_to_all x3 -> x11, starting transfers between devices: 21.3 us -> 69.3 us  [exchange(): return lax.all_to_all(blocks, axis, split_axis=0, concat_axis=0, tiled=True)]
    scatter-add x2 -> x0, other arithmetic: 20 us -> none  [the longest x1 13 us: body(): jax.ops.segment_sum(d_embeds.reshape(-1, width), positions.reshape(-1), n...]
  transfers between devices with their start and end apart: 11 -> 12, of which waited for: 11 -> 11; matrix products, arithmetic and copies ran while one was open for 5% -> 15% of each run, Pallas kernels for 0% -> 0%
where the time goes in v1:
time: 377 us; the launch traced here: 375 us
  waiting for transfers between devices  169 us (45%)
  starting transfers between devices  69.4 us (18%)
  blocking collectives  53.2 us (14%)
  matrix products  36 us (10%)
  local copies, waits for them, and re-layouts  19.7 us (5%)
  between operations  14.6 us (4%)
  other arithmetic  12.8 us (3%)
    all_to_all x11, waiting for transfers between devices, exchange(): return lax.all_to_all(blocks, axis, split_axis=0, concat_axis=0, tiled=True)  155 us
    all_to_all x11, starting transfers between devices, exchange(): return lax.all_to_all(blocks, axis, split_axis=0, concat_axis=0, tiled=True)  69.3 us
    all_to_all x2, blocking collectives, exchange(): return lax.all_to_all(blocks, axis, split_axis=0, concat_axis=0, tiled=True)  53.2 us
    all_gather x1, waiting for transfers between devices, body(): group_grads = lax.all_gather(grad_mlp, 'shard', axis=0, tiled=True)  14.6 us
  transfers between devices with their start and end apart: 12, of which 11 were waited for; matrix products, arithmetic and copies ran while one was open for 15% of the time, Pallas kernels for 0%

profile of v1, /device:TPU:1, one launch (start us, length us, event | category | flops | bytes accessed | tf_op | source)
XLA Modules:
  0.0 375.0 jit_solution(15082583750981058265)
XLA Ops:
  9.5 19.1 %all_to_all.69 = s32[32,1,32]{2,1,0:T(1,128)S(1)} all-to-all(s32[32,1,32]{2,1,0:T(1,128)} %bitcast.131), channel_id=1, replica_groups=mesh['dp'=16,'shard'=32] {'shard'}, dimensions={0} | all-to-all | bytes 8192 | tf_op jit(solution)/shard_map/all_to_all | solution.py:20
  33.0 3.9 %all-to-all-start.1 = ((bf16[32,32,160]{2,1,0:T(8,128)(2,1)}), bf16[32,32,160]{2,1,0:T(8,128)(2,1)S(1)}, u32[]{:S(2)}, u32[]{:S(2)}) async-start(bf16[32,32,160]{2,1,0:T(8,128)(2,1)} %bitcast.3), calls=%async_computation.1 | async-start | bytes 1048576 | tf_op jit(solution)/shard_map/all_to_all | solution.py:20
  37.0 15.5 %all-to-all-done.1 = bf16[32,32,160]{2,1,0:T(8,128)(2,1)S(1)} async-done(((bf16[32,32,160]{2,1,0:T(8,128)(2,1)}), bf16[32,32,160]{2,1,0:T(8,128)(2,1)S(1)}, u32[]{:S(2)}, u32[]{:S(2)}) %all-to-all-start.1) | async-done | bytes 327712 | tf_op jit(solution)/shard_map/all_to_all | solution.py:20
  59.8 34.1 %all_to_all.70 = bf16[32,16,1024]{2,1,0:T(8,128)(2,1)S(1)} all-to-all(bf16[32,16,1024]{2,1,0:T(8,128)(2,1)S(1)} %broadcast_in_dim.32), channel_id=1, replica_groups=mesh['dp'=16,'shard'=32] {'shard'}, dimensions={0} | all-to-all | bytes 2097152 | tf_op jit(solution)/shard_map/all_to_all | solution.py:20
  94.4 14.6 %all-gather.2.cloned.1.call-done = bf16[512,2560]{1,0:T(8,128)(2,1)} async-done(((bf16[16,2560]{1,0:T(8,128)(2,1)}), bf16[512,2560]{1,0:T(8,128)(2,1)}) %all-gather.2.cloned.1.call-update) | async-done | bytes 2621456 | tf_op jit(solution)/shard_map/all_gather | solution.py:48
  113.0 6.8 %all-to-all-start.4 = ((bf16[32,16,1024]{2,1,0:T(8,128)(2,1)}), bf16[32,16,1024]{2,1,0:T(8,128)(2,1)}, u32[]{:S(2)}, u32[]{:S(2)}) async-start(bf16[32,16,1024]{2,1,0:T(8,128)(2,1)} %bitcast.120), calls=%async_computation.4 | async-start | bytes 2097152 | tf_op jit(solution)/shard_map/all_to_all | solution.py:20
  124.6 19.3 %all-to-all-done.4 = bf16[32,16,1024]{2,1,0:T(8,128)(2,1)} async-done(((bf16[32,16,1024]{2,1,0:T(8,128)(2,1)}), bf16[32,16,1024]{2,1,0:T(8,128)(2,1)}, u32[]{:S(2)}, u32[]{:S(2)}) %all-to-all-start.4) | async-done | bytes 1048608 | tf_op jit(solution)/shard_map/all_to_all | solution.py:20
  144.0 16.0 %all-to-all-start.8 = ((bf16[16,64,128]{2,1,0:T(8,128)(2,1)}), bf16[16,64,128]{2,1,0:T(8,128)(2,1)S(1)}, u32[]{:S(2)}, u32[]{:S(2)}) async-start(bf16[16,64,128]{2,1,0:T(8,128)(2,1)} %bitcast.126), calls=%async_computation.8 | async-start | bytes 524288 | tf_op jit(solution)/shard_map/all_to_all | solution.py:20
  165.9 5.5 %convolution_bitcast_fusion.4 = f32[128,8]{1,0:T(8,128)S(1)} fusion(bf16[16,128,160]{1,0,2:T(8,128)(2,1)S(1)} %bitcast.123, f32[16,160,8]{0,2,1:T(8,128)S(1)} %copy.160), kind=kOutput, calls=%fused_computation.39 | convolution fusion | flops 31457280 | bytes 741376 | tf_op jit(solution)/shard_map/bfd,bdk->fk/dot_general | solution.py:132
  172.1 4.7 %all-to-all-start.10 = ((f32[32,4,128]{2,1,0:T(4,128)}), f32[32,4,128]{2,1,0:T(4,128)S(1)}, u32[]{:S(2)}, u32[]{:S(2)}) async-start(f32[32,4,128]{2,1,0:T(4,128)} %bitcast.28), calls=%async_computation.10 | async-start | bytes 131072 | tf_op jit(solution)/shard_map/all_to_all | solution.py:20
  180.2 5.5 %all-to-all-done.10 = f32[32,4,128]{2,1,0:T(4,128)S(1)} async-done(((f32[32,4,128]{2,1,0:T(4,128)}), f32[32,4,128]{2,1,0:T(4,128)S(1)}, u32[]{:S(2)}, u32[]{:S(2)}) %all-to-all-start.10) | async-done | bytes 65568 | tf_op jit(solution)/shard_map/all_to_all | solution.py:20
  186.3 8.8 %all-to-all-start.9 = ((bf16[16,160,128]{2,1,0:T(8,128)(2,1)}), bf16[16,160,128]{2,1,0:T(8,128)(2,1)S(1)}, u32[]{:S(2)}, u32[]{:S(2)}) async-start(bf16[16,160,128]{2,1,0:T(8,128)(2,1)} %bitcast.22), calls=%async_computation.9 | async-start | bytes 1310720 | tf_op jit(solution)/shard_map/all_to_all | solution.py:20
  200.7 14.4 %all-to-all-done.9 = bf16[16,160,128]{2,1,0:T(8,128)(2,1)S(1)} async-done(((bf16[16,160,128]{2,1,0:T(8,128)(2,1)}), bf16[16,160,128]{2,1,0:T(8,128)(2,1)S(1)}, u32[]{:S(2)}, u32[]{:S(2)}) %all-to-all-start.9) | async-done | bytes 655392 | tf_op jit(solution)/shard_map/all_to_all | solution.py:20
  221.5 4.6 %all-to-all-done.11 = f32[16,4,128]{2,1,0:T(4,128)S(1)} async-done(((f32[16,4,128]{2,1,0:T(4,128)}), f32[16,4,128]{2,1,0:T(4,128)S(1)}, u32[]{:S(2)}, u32[]{:S(2)}) %all-to-all-start.11) | async-done | bytes 32800 | tf_op jit(solution)/shard_map/all_to_all | solution.py:20
  226.1 3.9 %all-to-all-start.5 = ((bf16[32,32,160]{2,1,0:T(8,128)(2,1)}), bf16[32,32,160]{2,1,0:T(8,128)(2,1)S(1)}, u32[]{:S(2)}, u32[]{:S(2)}) async-start(bf16[32,32,160]{2,1,0:T(8,128)(2,1)} %fusion.19), calls=%async_computation.5 | async-start | bytes 1048576 | tf_op jit(solution)/shard_map/all_to_all | solution.py:20
  230.1 14.9 %all-to-all-done.5 = bf16[32,32,160]{2,1,0:T(8,128)(2,1)S(1)} async-done(((bf16[32,32,160]{2,1,0:T(8,128)(2,1)}), bf16[32,32,160]{2,1,0:T(8,128)(2,1)S(1)}, u32[]{:S(2)}, u32[]{:S(2)}) %all-to-all-start.5) | async-done | bytes 327712 | tf_op jit(solution)/shard_map/all_to_all | solution.py:20
  245.6 7.4 %all-to-all-start.12 = ((f32[32,4,128]{2,1,0:T(4,128)}), f32[32,4,128]{2,1,0:T(4,128)S(1)}, u32[]{:S(2)}, u32[]{:S(2)}) async-start(f32[32,4,128]{2,1,0:T(4,128)} %broadcast_in_dim.36), calls=%async_computation.12 | async-start | bytes 131072 | tf_op jit(solution)/shard_map/all_to_all | solution.py:20
  254.8 7.0 %all-to-all-done.12 = f32[32,4,128]{2,1,0:T(4,128)S(1)} async-done(((f32[32,4,128]{2,1,0:T(4,128)}), f32[32,4,128]{2,1,0:T(4,128)S(1)}, u32[]{:S(2)}, u32[]{:S(2)}) %all-to-all-start.12) | async-done | bytes 65568 | tf_op jit(solution)/shard_map/all_to_all | solution.py:20
  261.8 5.6 %all-to-all-start.6 = ((bf16[16,80,128]{2,1,0:T(8,128)(2,1)}), bf16[16,80,128]{2,1,0:T(8,128)(2,1)S(1)}, u32[]{:S(2)}, u32[]{:S(2)}) async-start(bf16[16,80,128]{2,1,0:T(8,128)(2,1)} %bitcast.17), calls=%async_computation.6 | async-start | bytes 655360 | tf_op jit(solution)/shard_map/all_to_all | solution.py:20
  269.8 10.7 %all-to-all-done.6 = bf16[16,80,128]{2,1,0:T(8,128)(2,1)S(1)} async-done(((bf16[16,80,128]{2,1,0:T(8,128)(2,1)}), bf16[16,80,128]{2,1,0:T(8,128)(2,1)S(1)}, u32[]{:S(2)}, u32[]{:S(2)}) %all-to-all-start.6) | async-done | bytes 327712 | tf_op jit(solution)/shard_map/all_to_all | solution.py:20
  281.2 4.1 %all-to-all-start.3 = ((bf16[32,16,2560]{2,1,0:T(8,128)(2,1)}), bf16[32,16,2560]{2,1,0:T(8,128)(2,1)S(1)}, u32[]{:S(2)}, u32[]{:S(2)}) async-start(bf16[32,16,2560]{2,1,0:T(8,128)(2,1)} %bitcast.115), calls=%async_computation.3 | async-start | bytes 5242880 | tf_op jit(solution)/shard_map/all_to_all | solution.py:20
  291.3 56.3 %all-to-all-done.3 = bf16[32,16,2560]{2,1,0:T(8,128)(2,1)S(1)} async-done(((bf16[32,16,2560]{2,1,0:T(8,128)(2,1)}), bf16[32,16,2560]{2,1,0:T(8,128)(2,1)S(1)}, u32[]{:S(2)}, u32[]{:S(2)}) %all-to-all-start.3) | async-done | bytes 2621472 | tf_op jit(solution)/shard_map/all_to_all | solution.py:20
  348.3 4.8 %all-to-all-start.7 = ((bf16[16,80,128]{2,1,0:T(8,128)(2,1)}), bf16[16,80,128]{2,1,0:T(8,128)(2,1)}, u32[]{:S(2)}, u32[]{:S(2)}) async-start(bf16[16,80,128]{2,1,0:T(8,128)(2,1)} %broadcast_in_dim.34), calls=%async_computation.7 | async-start | bytes 655360 | tf_op jit(solution)/shard_map/all_to_all | solution.py:20
  359.8 6.5 %all-to-all-done.7 = bf16[16,80,128]{2,1,0:T(8,128)(2,1)} async-done(((bf16[16,80,128]{2,1,0:T(8,128)(2,1)}), bf16[16,80,128]{2,1,0:T(8,128)(2,1)}, u32[]{:S(2)}, u32[]{:S(2)}) %all-to-all-start.7) | async-done | bytes 327712 | tf_op jit(solution)/shard_map/all_to_all | solution.py:20
  (153 shorter events, 66.5 us)
Async XLA Ops:
  7.2 101.8 %copy-start = (bf16[128,2560]{1,0:T(8,128)(2,1)S(1)}, bf16[128,2560]{1,0:T(8,128)(2,1)}, u32[]{:S(2)}) copy-start(bf16[128,2560]{1,0:T(8,128)(2,1)} %param.17) | copy-start | bytes 1966084
  7.2 101.8 %all-gather.2.cloned.1.call-start = ((), (), s32[]{:S(2)}) async-start(), calls=%async_computation.13 | async-start | bytes 2703360 | tf_op jit(solution)/shard_map/all_gather | solution.py:48
  29.9 22.8 %copy-start.37 = (s32[16,128]{1,0:T(8,128)S(1)}, s32[16,128]{1,0:T(8,128)}, u32[]{:S(2)}) copy-start(s32[16,128]{1,0:T(8,128)} %param.13) | copy-start | bytes 24580
  33.0 19.5 %all-to-all-start.1 = ((bf16[32,32,160]{2,1,0:T(8,128)(2,1)}), bf16[32,32,160]{2,1,0:T(8,128)(2,1)S(1)}, u32[]{:S(2)}, u32[]{:S(2)}) async-start(bf16[32,32,160]{2,1,0:T(8,128)(2,1)} %bitcast.3), calls=%async_computation.1 | async-start | bytes 1048576 | tf_op jit(solution)/shard_map/all_to_all | solution.py:20
  55.0 109.3 %copy-start.2 = (bf16[2048,160]{0,1:T(8,128)(2,1)}, bf16[2048,160]{0,1:T(8,128)(2,1)S(1)}, u32[]{:S(2)}) copy-start(bf16[2048,160]{0,1:T(8,128)(2,1)S(1)} %fusion.9) | copy-start | bytes 1966084
  58.8 35.1 %copy-start.9 = (f32[16,128,8]{1,2,0:T(8,128)}, f32[16,128,8]{1,2,0:T(8,128)S(1)}, u32[]{:S(2)}) copy-start(f32[16,128,8]{1,2,0:T(8,128)S(1)} %get-tuple-element.54) | copy-start | bytes 196612
  59.1 34.9 %copy-start.8 = (bf16[1024,128]{1,0:T(8,128)(2,1)S(1)}, bf16[1024,128]{1,0:T(8,128)(2,1)}, u32[]{:S(2)}) copy-start(bf16[1024,128]{1,0:T(8,128)(2,1)} %param.16) | copy-start | bytes 786436
  59.2 35.1 %copy-start.24 = (f32[16]{0:T(128)}, f32[16]{0:T(128)S(1)}, u32[]{:S(2)}) copy-start(f32[16]{0:T(128)S(1)} %broadcast_multiply_fusion.2) | copy-start | bytes 196
  59.5 34.8 %copy-start.27 = (f32[16]{0:T(128)}, f32[16]{0:T(128)S(1)}, u32[]{:S(2)}) copy-start(f32[16]{0:T(128)S(1)} %add_rsqrt_fusion) | copy-start | bytes 196
  113.0 31.0 %all-to-all-start.4 = ((bf16[32,16,1024]{2,1,0:T(8,128)(2,1)}), bf16[32,16,1024]{2,1,0:T(8,128)(2,1)}, u32[]{:S(2)}, u32[]{:S(2)}) async-start(bf16[32,16,1024]{2,1,0:T(8,128)(2,1)} %bitcast.120), calls=%async_computation.4 | async-start | bytes 2097152 | tf_op jit(solution)/shard_map/all_to_all | solution.py:20
  124.6 39.2 %copy-start.10 = (f32[16,128,8]{1,2,0:T(8,128)S(1)}, f32[16,128,8]{1,2,0:T(8,128)}, u32[]{:S(2)}) copy-start(f32[16,128,8]{1,2,0:T(8,128)} %copy-done.9) | copy-start | bytes 196612
  124.6 39.2 %copy-start.25 = (f32[16]{0:T(128)S(1)}, f32[16]{0:T(128)}, u32[]{:S(2)}) copy-start(f32[16]{0:T(128)} %copy-done.24) | copy-start | bytes 196
  124.6 39.2 %copy-start.28 = (f32[16]{0:T(128)S(1)}, f32[16]{0:T(128)}, u32[]{:S(2)}) copy-start(f32[16]{0:T(128)} %copy-done.27) | copy-start | bytes 196
  144.0 28.1 %all-to-all-start.8 = ((bf16[16,64,128]{2,1,0:T(8,128)(2,1)}), bf16[16,64,128]{2,1,0:T(8,128)(2,1)S(1)}, u32[]{:S(2)}, u32[]{:S(2)}) async-start(bf16[16,64,128]{2,1,0:T(8,128)(2,1)} %bitcast.126), calls=%async_computation.8 | async-start | bytes 524288 | tf_op jit(solution)/shard_map/all_to_all | solution.py:20
  172.1 13.6 %all-to-all-start.10 = ((f32[32,4,128]{2,1,0:T(4,128)}), f32[32,4,128]{2,1,0:T(4,128)S(1)}, u32[]{:S(2)}, u32[]{:S(2)}) async-start(f32[32,4,128]{2,1,0:T(4,128)} %bitcast.28), calls=%async_computation.10 | async-start | bytes 131072 | tf_op jit(solution)/shard_map/all_to_all | solution.py:20
  186.3 28.8 %all-to-all-start.9 = ((bf16[16,160,128]{2,1,0:T(8,128)(2,1)}), bf16[16,160,128]{2,1,0:T(8,128)(2,1)S(1)}, u32[]{:S(2)}, u32[]{:S(2)}) async-start(bf16[16,160,128]{2,1,0:T(8,128)(2,1)} %bitcast.22), calls=%async_computation.9 | async-start | bytes 1310720 | tf_op jit(solution)/shard_map/all_to_all | solution.py:20
  215.7 10.4 %all-to-all-start.11 = ((f32[16,4,128]{2,1,0:T(4,128)}), f32[16,4,128]{2,1,0:T(4,128)S(1)}, u32[]{:S(2)}, u32[]{:S(2)}) async-start(f32[16,4,128]{2,1,0:T(4,128)} %broadcast_in_dim.35), calls=%async_computation.11 | async-start | bytes 65536 | tf_op jit(solution)/shard_map/all_to_all | solution.py:20
  219.2 33.8 %copy-start.31 = (s32[1024]{0:T(1024)S(1)}, s32[1024]{0:T(1024)}, u32[]{:S(2)}) copy-start(s32[1024]{0:T(1024)} %copy-done.30) | copy-start | bytes 12292
  226.1 18.8 %all-to-all-start.5 = ((bf16[32,32,160]{2,1,0:T(8,128)(2,1)}), bf16[32,32,160]{2,1,0:T(8,128)(2,1)S(1)}, u32[]{:S(2)}, u32[]{:S(2)}) async-start(bf16[32,32,160]{2,1,0:T(8,128)(2,1)} %fusion.19), calls=%async_computation.5 | async-start | bytes 1048576 | tf_op jit(solution)/shard_map/all_to_all | solution.py:20
  245.6 16.3 %all-to-all-start.12 = ((f32[32,4,128]{2,1,0:T(4,128)}), f32[32,4,128]{2,1,0:T(4,128)S(1)}, u32[]{:S(2)}, u32[]{:S(2)}) async-start(f32[32,4,128]{2,1,0:T(4,128)} %broadcast_in_dim.36), calls=%async_computation.12 | async-start | bytes 131072 | tf_op jit(solution)/shard_map/all_to_all | solution.py:20
  261.8 18.7 %all-to-all-start.6 = ((bf16[16,80,128]{2,1,0:T(8,128)(2,1)}), bf16[16,80,128]{2,1,0:T(8,128)(2,1)S(1)}, u32[]{:S(2)}, u32[]{:S(2)}) async-start(bf16[16,80,128]{2,1,0:T(8,128)(2,1)} %bitcast.17), calls=%async_computation.6 | async-start | bytes 655360 | tf_op jit(solution)/shard_map/all_to_all | solution.py:20
  281.2 66.4 %all-to-all-start.3 = ((bf16[32,16,2560]{2,1,0:T(8,128)(2,1)}), bf16[32,16,2560]{2,1,0:T(8,128)(2,1)S(1)}, u32[]{:S(2)}, u32[]{:S(2)}) async-start(bf16[32,16,2560]{2,1,0:T(8,128)(2,1)} %bitcast.115), calls=%async_computation.3 | async-start | bytes 5242880 | tf_op jit(solution)/shard_map/all_to_all | solution.py:20
  288.4 66.7 %copy-start.16 = (f32[32,4,128]{2,1,0:T(4,128)S(1)}, f32[32,4,128]{2,1,0:T(4,128)}, u32[]{:S(2)}) copy-start(f32[32,4,128]{2,1,0:T(4,128)} %copy-done.15) | copy-start | bytes 196612
  348.3 18.0 %all-to-all-start.7 = ((bf16[16,80,128]{2,1,0:T(8,128)(2,1)}), bf16[16,80,128]{2,1,0:T(8,128)(2,1)}, u32[]{:S(2)}, u32[]{:S(2)}) async-start(bf16[16,80,128]{2,1,0:T(8,128)(2,1)} %broadcast_in_dim.34), calls=%async_computation.7 | async-start | bytes 655360 | tf_op jit(solution)/shard_map/all_to_all | solution.py:20
  (27 other events, 181.7 us)
Sparse Core Ops, SparseCore 0:
  11.2 97.7 all-gather.1

commit v2 on v1

v2 whole, which is shorter than its diff:
```python
import jax
import jax.numpy as jnp
from jax import lax
from jax.experimental import pallas as pl
from jax.experimental.pallas import tpu as pltpu
from jax.sharding import PartitionSpec as P

F = 128
K = 8
NF = 16
CAP = 32
LANES = 128


def layer_norm(flat):
    center = flat - jnp.mean(flat, axis=1, keepdims=True)
    inverse_std = lax.rsqrt(jnp.mean(center * center, axis=1, keepdims=True) + 1e-05)
    return (center * inverse_std, inverse_std)


def exchange(blocks, axis):
    return lax.all_to_all(blocks, axis, split_axis=0, concat_axis=0, tiled=True)


def spread(block, axis):
    count = lax.axis_size(axis)
    return exchange(jnp.broadcast_to(block[None], (count, *block.shape)), axis)


def gather(block, axis):
    return lax.all_gather(block, axis, axis=0, tiled=True)


def scatter(blocks, axis):
    return lax.psum_scatter(blocks, axis, scatter_dimension=0, tiled=True)


def halves(value):
    high = lax.reduce_precision(value, 8, 7)
    return jnp.concatenate([high, value - high], axis=-1).astype(jnp.bfloat16)


def network_kernel(ring, weights, lcb, back, activ, d_pre):
    f32, bf16 = jnp.float32, jnp.bfloat16
    split, end = F * K, weights.shape[1]
    cross = (((1,), (1,)), ((), ()))
    preact = lax.dot_general(
        ring[:, :split], weights[:, :split], cross, preferred_element_type=f32
    )
    d_hidden = lax.dot_general(
        ring[:, split:], weights[:, split:], cross, preferred_element_type=f32
    )
    sigmoid = 1.0 / (1.0 + jnp.exp(-preact))
    activ[...] = (preact * sigmoid).astype(bf16)
    d_pre[...] = (d_hidden * sigmoid * (1.0 + preact * (1.0 - sigmoid))).astype(bf16)
    back[:, :split] = jnp.dot(
        d_pre[...], weights[:, :split], preferred_element_type=f32
    ).astype(bf16)
    for start in range(split, end, 512):
        columns = slice(start, start + 512)
        back[:, columns] = jnp.dot(
            activ[...], weights[:, columns], preferred_element_type=f32
        ).astype(bf16)
    back[:, end:] = lcb[...]


def network(ring, weights, lcb):
    samples, taps = ring.shape[0], weights.shape[0]
    columns = weights.shape[1] + lcb.shape[1]
    return pl.pallas_call(
        network_kernel,
        out_shape=(
            jax.ShapeDtypeStruct((samples, columns), jnp.bfloat16),
            jax.ShapeDtypeStruct((samples, taps), jnp.bfloat16),
            jax.ShapeDtypeStruct((samples, taps), jnp.bfloat16),
        ),
        compiler_params=pltpu.CompilerParams(vmem_limit_bytes=32 * 2**20),
        cost_estimate=pl.CostEstimate(
            flops=4 * samples * taps * columns, bytes_accessed=6_000_000, transcendentals=65536
        ),
    )(ring, weights, lcb)


def weight_kernel(me, ring, activ, d_pre, keep, send):
    _, depth, _, _ = keep.shape
    first = me[0] == 0
    split = F * K
    start = 0
    for begin, end, right in ((split, ring.shape[1], activ), (0, split, d_pre)):
        rows = (end - begin) // (2 * depth)
        for z in range(depth):
            at = begin + z * 2 * rows
            part = lax.dot_general(
                ring[:, at : at + 2 * rows],
                right[...],
                (((0,), (0,)), ((), ())),
                preferred_element_type=jnp.float32,
            )
            low, high = part[:rows], part[rows:]
            here = slice(start, start + rows)
            keep[0, z, here] = jnp.where(first, low, high).astype(jnp.bfloat16)
            send[0, z, here] = jnp.where(first, high, low).astype(jnp.bfloat16)
        start += rows


def weight_products(ring, activ, d_pre, hidden, depth):
    samples = ring.shape[0]
    far = activ.shape[1] // hidden
    rows = ring.shape[1] // (2 * depth)
    chunk = pl.BlockSpec((samples, hidden), lambda j: (0, j))
    half = pl.BlockSpec((1, depth, rows, hidden), lambda j: (j, 0, 0, 0))
    shape = jax.ShapeDtypeStruct((far, depth, rows, hidden), jnp.bfloat16)
    return pl.pallas_call(
        weight_kernel,
        grid=(far,),
        in_specs=[
            pl.BlockSpec(memory_space=pltpu.SMEM),
            pl.BlockSpec(ring.shape, lambda j: (0, 0)),
            chunk,
            chunk,
        ],
        out_specs=(half, half),
        out_shape=(shape, shape),
        compiler_params=pltpu.CompilerParams(vmem_limit_bytes=32 * 2**20),
        cost_estimate=pl.CostEstimate(
            flops=4 * samples * rows * depth * far * hidden,
            bytes_accessed=6_000_000,
            transcendentals=0,
        ),
    )(lax.axis_index("core").reshape(1), ring, activ, d_pre)


def body(
    table, slot_rows, slot_counts, positions, fm_proj, ln_gain, w_up, w_down, w_lcb, cotangent
):
    highest = lax.Precision.HIGHEST
    f32, bf16 = jnp.float32, jnp.bfloat16
    shard, dp = ("x", "y"), ("z", "core")
    far, near = lax.axis_size("x"), lax.axis_size("y")
    depth, cores = lax.axis_size("z"), lax.axis_size("core")
    members, groups = far * near, depth * cores
    batch = positions.shape[0]
    width = table.shape[1]
    rows_here = table.shape[0]
    slots = members * CAP
    hidden = w_up.shape[1]
    request = slot_rows.reshape(members, CAP)
    counts_here = slot_counts.reshape(members)

    grad_mlp = cotangent[:, :NF, :].reshape(batch, NF * width)
    weights = gather(jnp.concatenate([w_up.T, w_down], axis=1), "x")

    asked = exchange(request, shard).reshape(slots)
    row_ids = lax.broadcasted_iota(jnp.int32, (slots, rows_here), 1)
    asked_hot = (asked[:, None] == row_ids).astype(bf16)
    sent = jnp.dot(asked_hot, table, preferred_element_type=f32).astype(bf16)
    fetched = exchange(sent.reshape(members, CAP, width), shard)
    live_mask = lax.broadcasted_iota(jnp.int32, (members, CAP), 1) < counts_here[:, None]
    fetched = jnp.where(live_mask[:, :, None], fetched, jnp.zeros((), bf16)).reshape(slots, width)
    flat_positions = positions.reshape(batch * F)
    slot_ids = lax.broadcasted_iota(jnp.int32, (batch * F, slots), 1)
    slot_hot = (flat_positions[:, None] == slot_ids).astype(bf16)
    embeds = jnp.dot(slot_hot, fetched, preferred_element_type=f32).astype(bf16)
    embeds = embeds.reshape(batch, F, width)

    embeds_f = embeds.astype(f32)
    projector = fm_proj.astype(f32)
    compressed = jnp.einsum("bfd,fk->bdk", embeds, fm_proj, preferred_element_type=f32)
    gram = jnp.einsum("bfd,bdk->bfk", embeds_f, compressed, precision=highest).reshape(batch, F * K)
    normal_part, inverse_std = layer_norm(gram)
    normed = (normal_part * ln_gain).astype(bf16)
    ring = spread(jnp.concatenate([normed, grad_mlp], axis=1), "y")
    ring = ring.reshape(near * batch, -1)

    grad_linear = cotangent[:, NF:, :]
    linear_part = jnp.einsum("lf,bfd->bld", w_lcb, embeds, preferred_element_type=f32)
    lcb_part = jnp.einsum("bld,bfd->lf", grad_linear, embeds, preferred_element_type=f32)
    lcb_part = lcb_part.astype(bf16).reshape(near * batch, -1)
    spare = -lcb_part.shape[1] % LANES
    back, activ, d_pre = network(ring, weights, jnp.pad(lcb_part, ((0, 0), (0, spare))))
    back = exchange(back.reshape(near, batch, -1), "y")
    keep, send = weight_products(ring, activ, d_pre, hidden, depth)
    other = lax.ppermute(send, "core", [(0, 1), (1, 0)])
    weight_sum = (keep.astype(f32) + other.astype(f32)).astype(bf16).reshape(-1, hidden)
    back, weight_sum = lax.optimization_barrier((back, weight_sum))
    weight_sum = scatter(weight_sum, "x")
    back = jnp.sum(back.astype(f32), axis=0)
    split, end = F * K, F * K + NF * width
    d_normed, mlp_out = back[:, :split], back[:, split:end]
    lcb_mine = back[:, end : end + lcb_part.shape[1]].astype(bf16)
    d_linear = jnp.einsum("lf,bld->bfd", w_lcb, grad_linear, preferred_element_type=f32)

    gain_part = jnp.sum(d_normed * normal_part, axis=0)
    scaled = d_normed * ln_gain
    d_gram = inverse_std * (
        scaled
        - jnp.mean(scaled, axis=1, keepdims=True)
        - normal_part * jnp.mean(scaled * normal_part, axis=1, keepdims=True)
    )
    d_gram = d_gram.reshape(batch, F, K)
    d_compressed = jnp.einsum("bfd,bfk->bdk", embeds_f, d_gram, precision=highest)
    d_embeds = cotangent.astype(f32) + d_linear
    d_embeds = d_embeds + jnp.einsum("bfk,bdk->bfd", d_gram, compressed, precision=highest)
    d_embeds = d_embeds + jnp.einsum("fk,bdk->bfd", projector, d_compressed, precision=highest)
    d_embeds = d_embeds.astype(bf16).reshape(batch * F, width)
    slot_rows_hot = (
        lax.broadcasted_iota(jnp.int32, (slots, batch * F), 0) == flat_positions[None, :]
    ).astype(bf16)
    slot_grad = jnp.dot(slot_rows_hot, d_embeds, preferred_element_type=f32)
    slot_grad = slot_grad.reshape(members, CAP, width)
    slot_grad = jnp.where(live_mask[:, :, None], slot_grad, 0.0).astype(bf16)
    proj_part = jnp.einsum("bfd,bdk->fk", embeds, halves(d_compressed), preferred_element_type=f32)
    proj_part = proj_part[:, :K] + proj_part[:, K:]
    small = jnp.concatenate([gain_part, proj_part.reshape(-1)]).astype(bf16).reshape(CAP, -1)
    row = 2 * LANES
    lcb_mine = lcb_mine.reshape(-1, row)
    lcb_mine = jnp.pad(lcb_mine, ((0, -lcb_mine.shape[0] % 8), (0, 0)))
    small = jnp.pad(small, ((0, 0), (0, row - width - small.shape[1])))
    sent = jnp.concatenate([slot_grad, jnp.broadcast_to(small[None], (members, *small.shape))], axis=2)
    lcb_sent = jnp.broadcast_to(lcb_mine[None], (members, *lcb_mine.shape))
    received = exchange(jnp.concatenate([sent, lcb_sent], axis=1), shard)
    received, weight_sum = lax.optimization_barrier((received, weight_sum))
    weight_sum = scatter(weight_sum, "z")
    returned = received[:, :CAP, :width].reshape(slots, width)
    small_end = width + 2 * F * K // CAP
    small = jnp.sum(received[:, :CAP, width:small_end].astype(f32), axis=0).astype(bf16)
    lcb = received[:, CAP:].reshape(far, near, -1)[:, :, : (F - NF) * F // near]
    lcb = jnp.sum(lcb.astype(f32), axis=0).astype(bf16)
    small = jnp.concatenate([small.reshape(-1), lcb.reshape(-1)]).reshape(groups, -1, LANES)
    row_hot = (
        lax.broadcasted_iota(jnp.int32, (rows_here, slots), 0) == asked[None, :]
    ).astype(bf16)
    table_part = lax.dot_general(
        returned, row_hot, (((0,), (1,)), ((), ())), preferred_element_type=f32
    ).astype(bf16)
    columns = rows_here // LANES
    table_part = table_part.reshape(width, columns, LANES).transpose(1, 0, 2)
    table_part = table_part.reshape(groups, -1, LANES)
    held = table_part.shape[1]
    total = exchange(jnp.concatenate([table_part, small], axis=1), dp)
    total = spread(jnp.sum(total.astype(f32), axis=0).astype(bf16), dp)
    total, weight_sum = lax.optimization_barrier((total, weight_sum))
    down_count = NF * width // groups
    grad_w_down = weight_sum[:down_count].T
    grad_w_up = weight_sum[down_count:]
    table_all = total[:, :held].reshape(columns, width, LANES)
    grad_table = table_all.transpose(0, 2, 1).reshape(rows_here, width).astype(f32)
    small = total[:, held:].reshape(-1).astype(f32)
    grad_ln_gain = small[: F * K]
    grad_fm_proj = small[F * K : 2 * F * K].reshape(F, K)
    grad_w_lcb = small[2 * F * K :].reshape(F - NF, F)

    joined = jnp.concatenate([mlp_out.reshape(batch, NF, width), linear_part], axis=1)
    mixed = (embeds_f + joined).astype(bf16)
    return (mixed, grad_table, grad_w_up, grad_w_down, grad_fm_proj, grad_w_lcb, grad_ln_gain)


def solution(mesh):
    dp, shard = mesh.devices.shape
    near = min(8, shard // 2)
    split = (dp // 2, 2, shard // near, near)
    mesh = jax.sharding.Mesh(mesh.devices.reshape(split), ("z", "core", "x", "y"))
    dp, shard = ("z", "core"), ("x", "y")
    every = (*dp, *shard)
    placed = (
        P(shard, None),
        P(dp, shard, None, None),
        P(dp, shard, None),
        P(every, None),
        P(),
        P(),
        P(None, shard),
        P(shard, None),
        P(),
        P(every, None, None),
    )
    return jax.shard_map(
        body,
        mesh=mesh,
        in_specs=placed,
        out_specs=(
            P(every, None, None),
            P(shard, None),
            P(dp, shard),
            P(shard, dp),
            P(),
            P(),
            P(),
        ),
        check_vma=False,
    )
```

time: 377 us -> 240 us (0.64)
  the two profiles are of different devices: /device:TPU:1 before, /device:TPU:8 now
where the time goes in v2:
time: 240 us; the launch traced here: 239 us
  waiting for transfers between devices  89 us (37%)
  blocking collectives  44.1 us (18%)
  starting transfers between devices  30.5 us (13%)
  matrix products  21.9 us (9%)
  local copies, waits for them, and re-layouts  19.2 us (8%)
  other arithmetic  14.5 us (6%)
  between operations  14.3 us (6%)
  Pallas kernels  5.59 us (2%)
    all_to_all x5, waiting for transfers between devices, exchange(): return lax.all_to_all(blocks, axis, split_axis=0, concat_axis=0, tiled=True)  66.8 us
    all_to_all x2, blocking collectives, exchange(): return lax.all_to_all(blocks, axis, split_axis=0, concat_axis=0, tiled=True)  44.1 us
    all_to_all x5, starting transfers between devices, exchange(): return lax.all_to_all(blocks, axis, split_axis=0, concat_axis=0, tiled=True)  28.5 us
    reduce_scatter x2, waiting for transfers between devices, scatter(): return lax.psum_scatter(blocks, axis, scatter_dimension=0, tiled=True)  21.5 us
    unnamed x52, local copies, waits for them, and re-layouts  5.66 us
  transfers between devices with their start and end apart: 9, of which 5 were waited for; matrix products, arithmetic and copies ran while one was open for 16% of the time, Pallas kernels for 0%

profile of v2, /device:TPU:8, one launch (start us, length us, event | category | flops | bytes accessed | tf_op | source)
XLA Modules:
  0.0 239.1 jit_solution(11159100941936034304)
XLA Ops:
  8.4 2.1 pad_maximum_fusion
  10.5 18.6 %all_to_all.39 = s32[32,1,32]{2,1,0:T(1,128)S(1)} all-to-all(s32[32,1,32]{2,1,0:T(1,128)S(1)} %bitcast.132), channel_id=1, replica_groups=mesh['z'=8,'core'=2,'x'=4,'y'=8] {'x','y'}, dimensions={0} | all-to-all | bytes 8192 | tf_op jit(solution)/shard_map/all_to_all | solution.py:22
  32.5 5.0 %all-to-all-start.1 = ((bf16[32,32,160]{2,1,0:T(8,128)(2,1)}), bf16[32,32,160]{2,1,0:T(8,128)(2,1)S(1)}, u32[]{:S(2)}, u32[]{:S(2)}) async-start(bf16[32,32,160]{2,1,0:T(8,128)(2,1)} %bitcast.3), calls=%async_computation.1 | async-start | bytes 1048576 | tf_op jit(solution)/shard_map/all_to_all | solution.py:22
  38.0 16.0 %all-to-all-done.1 = bf16[32,32,160]{2,1,0:T(8,128)(2,1)S(1)} async-done(((bf16[32,32,160]{2,1,0:T(8,128)(2,1)}), bf16[32,32,160]{2,1,0:T(8,128)(2,1)S(1)}, u32[]{:S(2)}, u32[]{:S(2)}) %all-to-all-start.1) | async-done | bytes 327712 | tf_op jit(solution)/shard_map/all_to_all | solution.py:22
  54.3 2.3 fusion.8
  61.4 3.9 %all-to-all-start.2 = ((bf16[8,16,3584]{2,1,0:T(8,128)(2,1)}), bf16[8,16,3584]{2,1,0:T(8,128)(2,1)S(1)}, u32[]{:S(2)}, u32[]{:S(2)}) async-start(bf16[8,16,3584]{2,1,0:T(8,128)(2,1)} %broadcast_in_dim.32), calls=%async_computation.2 | async-start | bytes 1835008 | tf_op jit(solution)/shard_map/all_to_all | solution.py:22
  68.0 18.9 %all-to-all-done.2 = bf16[8,16,3584]{2,1,0:T(8,128)(2,1)S(1)} async-done(((bf16[8,16,3584]{2,1,0:T(8,128)(2,1)}), bf16[8,16,3584]{2,1,0:T(8,128)(2,1)S(1)}, u32[]{:S(2)}, u32[]{:S(2)}) %all-to-all-start.2) | async-done | bytes 917536 | tf_op jit(solution)/shard_map/all_to_all | solution.py:22
  86.9 2.0 copy-done.1
  88.9 1.9 shard_map.153
  90.9 3.7 %shard_map.154 = (bf16[4,8,224,128]{3,2,1,0:T(8,128)(2,1)S(1)}, bf16[4,8,224,128]{3,2,1,0:T(8,128)(2,1)}) custom-call(s32[1]{0:T(128)} %bitcast.12.me, bf16[128,3584]{1,0:T(8,128)(2,1)S(1)} %bitcast.115, bf16[128,512]{1,0:T(8,128)(2,1)S(1)} %get-tuple-element.19.activ, bf16[128,512]{1,0:T(8,128)(2,1)S(1)} %get-tuple-element.20.d_pre), custom_call_target="tpu_custom_call" | custom-call | flops 469762048 | bytes 6000000 | tf_op jit(solution)/shard_map/pallas_call | solution.py:113
  94.6 1.9 collective-permute-start
  96.5 5.6 %all-to-all-start.3 = ((bf16[8,16,3712]{2,1,0:T(8,128)(2,1)}), bf16[8,16,3712]{2,1,0:T(8,128)(2,1)}, u32[]{:S(2)}, u32[]{:S(2)}) async-start(bf16[8,16,3712]{2,1,0:T(8,128)(2,1)} %bitcast.116), calls=%async_computation.3 | async-start | bytes 1900544 | tf_op jit(solution)/shard_map/all_to_all | solution.py:22
  102.7 2.8 %fusion.12 = f32[16,128,160]{1,2,0:T(8,128)} fusion(bf16[16,128,160]{1,2,0:T(8,128)(2,1)} %param.19, bf16[112,128]{1,0:T(8,128)(2,1)S(1)} %copy-done.9), kind=kOutput, calls=%fused_computation.20 | convolution fusion | flops 74055680 | bytes 2650112 | tf_op jit(solution)/shard_map/lf,bld->bfd/dot_general | solution.py:191
  105.5 3.2 %add_convert_fusion = bf16[4,8,224,128]{3,2,1,0:T(8,128)(2,1)} fusion(bf16[4,8,224,128]{3,2,1,0:T(8,128)(2,1)} %collective-permute-done, bf16[4,8,224,128]{3,2,1,0:T(8,128)(2,1)S(1)} %get-tuple-element.21), kind=kLoop, calls=%fused_computation.11 | loop fusion | flops 3670016 | bytes 5505024 | tf_op jit(solution)/shard_map/convert_element_type | solution.py:184
  108.8 19.6 %all-to-all-done.3 = bf16[8,16,3712]{2,1,0:T(8,128)(2,1)} async-done(((bf16[8,16,3712]{2,1,0:T(8,128)(2,1)}), bf16[8,16,3712]{2,1,0:T(8,128)(2,1)}, u32[]{:S(2)}, u32[]{:S(2)}) %all-to-all-start.3) | async-done | bytes 950304 | tf_op jit(solution)/shard_map/all_to_all | solution.py:22
  131.6 1.8 reduce-precision_convert_fusion
  137.4 2.1 convolution_bitcast_fusion
  139.5 2.3 fusion.13
  144.5 25.5 %all_to_all.40 = bf16[32,40,256]{2,1,0:T(8,128)(2,1)S(1)} all-to-all(bf16[32,40,256]{2,1,0:T(8,128)(2,1)S(1)} %pad_maximum_fusion.1), channel_id=1, replica_groups=mesh['z'=8,'core'=2,'x'=4,'y'=8] {'x','y'}, dimensions={0} | all-to-all | bytes 1310720 | tf_op jit(solution)/shard_map/all_to_all | solution.py:22
  172.4 10.4 %all-to-all-start.5 = ((bf16[16,88,128]{2,1,0:T(8,128)(2,1)}), bf16[16,88,128]{2,1,0:T(8,128)(2,1)S(1)}, u32[]{:S(2)}, u32[]{:S(2)}) async-start(bf16[16,88,128]{2,1,0:T(8,128)(2,1)} %pad_maximum_fusion.2), calls=%async_computation.6 | async-start | bytes 720896 | tf_op jit(solution)/shard_map/all_to_all | solution.py:22
  183.5 12.3 %all-to-all-done.5 = bf16[16,88,128]{2,1,0:T(8,128)(2,1)S(1)} async-done(((bf16[16,88,128]{2,1,0:T(8,128)(2,1)}), bf16[16,88,128]{2,1,0:T(8,128)(2,1)S(1)}, u32[]{:S(2)}, u32[]{:S(2)}) %all-to-all-start.5) | async-done | bytes 360480 | tf_op jit(solution)/shard_map/all_to_all | solution.py:22
  196.7 3.7 %all-to-all-start.6 = ((bf16[16,88,128]{2,1,0:T(8,128)(2,1)}), bf16[16,88,128]{2,1,0:T(8,128)(2,1)S(1)}, u32[]{:S(2)}, u32[]{:S(2)}) async-start(bf16[16,88,128]{2,1,0:T(8,128)(2,1)} %broadcast_in_dim.36), calls=%async_computation.7 | async-start | bytes 720896 | tf_op jit(solution)/shard_map/all_to_all | solution.py:22
  202.4 2.6 %fusion.14 = bf16[16,128,160]{1,2,0:T(8,128)(2,1)} fusion(f32[16,112,160]{1,2,0:T(8,128)} %convolution_bitcast_fusion.2, f32[16,16,160]{1,2,0:T(8,128)S(1)} %copy.82, bf16[2048,160]{0,1:T(8,128)(2,1)S(1)} %copy-done.7), kind=kLoop, calls=%fused_computation.24 | loop fusion | flops 1310720 | bytes 2621440 | tf_op jit(solution)/shard_map/convert_element_type | solution.py:254
  205.0 21.5 %reduce-scatter.5.cloned.1.call-done = bf16[224,128]{1,0:T(8,128)(2,1)} async-done(((bf16[1792,128]{1,0:T(8,128)(2,1)}), bf16[224,128]{1,0:T(8,128)(2,1)}) %reduce-scatter.5.cloned.1.call-update) | async-done | bytes 57360 | tf_op jit(solution)/shard_map/reduce_scatter | solution.py:35
  (134 shorter events, 35.0 us)
Async XLA Ops:
  7.2 23.2 %copy-start = (bf16[1024,160]{0,1:T(8,128)(2,1)S(1)}, bf16[1024,160]{0,1:T(8,128)(2,1)}, u32[]{:S(2)}) copy-start(bf16[1024,160]{0,1:T(8,128)(2,1)} %param.10) | copy-start | bytes 983044
  7.2 3.3 %copy-start.11 = (s32[1,1,32,32]{3,2,1,0:T(8,128)S(1)}, s32[1,1,32,32]{3,2,1,0:T(8,128)}, u32[]{:S(2)}) copy-start(s32[1,1,32,32]{3,2,1,0:T(8,128)} %param.11) | copy-start | bytes 12292
  7.2 79.7 %all-gather.2.cloned.1.call-start = ((), (), s32[]{:S(2)}) async-start(), calls=%async_computation.9 | async-start | bytes 4587520 | tf_op jit(solution)/shard_map/all_gather | solution.py:31
  30.4 7.1 %copy-start.5 = (bf16[16,128,160]{1,2,0:T(8,128)(2,1)S(1)}, bf16[16,128,160]{1,2,0:T(8,128)(2,1)}, u32[]{:S(2)}) copy-start(bf16[16,128,160]{1,2,0:T(8,128)(2,1)} %param.19) | copy-start | bytes 1966084
  31.5 6.5 %copy-start.21 = (s32[1,1,32]{2,1,0:T(1,128)S(1)}, s32[1,1,32]{2,1,0:T(1,128)}, u32[]{:S(2)}) copy-start(s32[1,1,32]{2,1,0:T(1,128)} %param.12) | copy-start | bytes 388
  31.5 22.8 %copy-start.22 = (s32[16,128]{1,0:T(8,128)S(1)}, s32[16,128]{1,0:T(8,128)}, u32[]{:S(2)}) copy-start(s32[16,128]{1,0:T(8,128)} %param.13) | copy-start | bytes 24580
  32.5 21.6 %all-to-all-start.1 = ((bf16[32,32,160]{2,1,0:T(8,128)(2,1)}), bf16[32,32,160]{2,1,0:T(8,128)(2,1)S(1)}, u32[]{:S(2)}, u32[]{:S(2)}) async-start(bf16[32,32,160]{2,1,0:T(8,128)(2,1)} %bitcast.3), calls=%async_computation.1 | async-start | bytes 1048576 | tf_op jit(solution)/shard_map/all_to_all | solution.py:22
  56.8 9.6 %copy-start.3 = (bf16[20,8,16,128]{3,2,1,0:T(8,128)(2,1)}, bf16[20,8,16,128]{3,2,1,0:T(8,128)(2,1)S(1)}, u32[]{:S(2)}) copy-start(bf16[20,8,16,128]{3,2,1,0:T(8,128)(2,1)S(1)} %copy.98) | copy-start | bytes 1966084
  56.8 3.4 %copy-start.10 = (f32[1024]{0:T(1024)S(1)}, f32[1024]{0:T(1024)}, u32[]{:S(2)}) copy-start(f32[1024]{0:T(1024)} %param.15) | copy-start | bytes 12292
  59.9 69.8 %copy-start.15 = (f32[16]{0:T(128)}, f32[16]{0:T(128)S(1)}, u32[]{:S(2)}) copy-start(f32[16]{0:T(128)S(1)} %broadcast_multiply_fusion.2) | copy-start | bytes 196
  60.2 69.5 %copy-start.17 = (f32[16]{0:T(128)}, f32[16]{0:T(128)S(1)}, u32[]{:S(2)}) copy-start(f32[16]{0:T(128)S(1)} %add_rsqrt_fusion) | copy-start | bytes 196
  61.4 25.5 %all-to-all-start.2 = ((bf16[8,16,3584]{2,1,0:T(8,128)(2,1)}), bf16[8,16,3584]{2,1,0:T(8,128)(2,1)S(1)}, u32[]{:S(2)}, u32[]{:S(2)}) async-start(bf16[8,16,3584]{2,1,0:T(8,128)(2,1)} %broadcast_in_dim.32), calls=%async_computation.2 | async-start | bytes 1835008 | tf_op jit(solution)/shard_map/all_to_all | solution.py:22
  90.8 5.6 %copy-start.2 = (bf16[128,3712]{1,0:T(8,128)(2,1)}, bf16[128,3712]{1,0:T(8,128)(2,1)S(1)}, u32[]{:S(2)}) copy-start(bf16[128,3712]{1,0:T(8,128)(2,1)S(1)} %get-tuple-element.18) | copy-start | bytes 2850820
  90.9 11.9 %copy-start.9 = (bf16[112,128]{1,0:T(8,128)(2,1)S(1)}, bf16[112,128]{1,0:T(8,128)(2,1)}, u32[]{:S(2)}) copy-start(bf16[112,128]{1,0:T(8,128)(2,1)} %param.18) | copy-start | bytes 86020
  94.6 10.9 %collective-permute-start = (bf16[4,8,224,128]{3,2,1,0:T(8,128)(2,1)}, bf16[4,8,224,128]{3,2,1,0:T(8,128)(2,1)}, u32[]{:S(2)}, u32[]{:S(2)}) collective-permute-start(bf16[4,8,224,128]{3,2,1,0:T(8,128)(2,1)} %get-tuple-element.22), channel_id=1, source_target_pairs={{0,32},{32,0},{1,33},{33,1},{2,34},{34,2},{3,35},{35,3},{4,36},{36... | collective-permute-start | bytes 5505032 | tf_op jit(solution)/shard_map/ppermute | solution.py:183
  96.5 31.9 %all-to-all-start.3 = ((bf16[8,16,3712]{2,1,0:T(8,128)(2,1)}), bf16[8,16,3712]{2,1,0:T(8,128)(2,1)}, u32[]{:S(2)}, u32[]{:S(2)}) async-start(bf16[8,16,3712]{2,1,0:T(8,128)(2,1)} %bitcast.116), calls=%async_computation.3 | async-start | bytes 1900544 | tf_op jit(solution)/shard_map/all_to_all | solution.py:22
  102.1 67.9 %reduce-scatter.3.cloned.1.call-start = ((), (), s32[]{:S(2)}) async-start(), calls=%async_computation.10 | async-start | bytes 2293760 | tf_op jit(solution)/shard_map/reduce_scatter | solution.py:35
  130.4 4.4 %copy-start.4 = (bf16[20,8,16,128]{3,2,1,0:T(8,128)(2,1)S(1)}, bf16[20,8,16,128]{3,2,1,0:T(8,128)(2,1)}, u32[]{:S(2)}) copy-start(bf16[20,8,16,128]{3,2,1,0:T(8,128)(2,1)} %copy-done.3) | copy-start | bytes 1966084
  131.6 5.8 %copy-start.14 = (bf16[128,8]{0,1:T(8,128)(2,1)S(1)}, bf16[128,8]{0,1:T(8,128)(2,1)}, u32[]{:S(2)}) copy-start(bf16[128,8]{0,1:T(8,128)(2,1)} %param.14) | copy-start | bytes 6148
  133.4 6.1 %copy-start.8 = (f32[16,128,160]{1,2,0:T(8,128)S(1)}, f32[16,128,160]{1,2,0:T(8,128)}, u32[]{:S(2)}) copy-start(f32[16,128,160]{1,2,0:T(8,128)} %fusion.12) | copy-start | bytes 3932164
  144.3 26.0 %copy-start.20 = (s32[1024]{0:T(1024)S(1)}, s32[1024]{0:T(1024)}, u32[]{:S(2)}) copy-start(s32[1024]{0:T(1024)} %copy-done.19) | copy-start | bytes 12292
  172.4 23.5 %all-to-all-start.5 = ((bf16[16,88,128]{2,1,0:T(8,128)(2,1)}), bf16[16,88,128]{2,1,0:T(8,128)(2,1)S(1)}, u32[]{:S(2)}, u32[]{:S(2)}) async-start(bf16[16,88,128]{2,1,0:T(8,128)(2,1)} %pad_maximum_fusion.2), calls=%async_computation.6 | async-start | bytes 720896 | tf_op jit(solution)/shard_map/all_to_all | solution.py:22
  182.8 43.6 %reduce-scatter.5.cloned.1.call-start = ((), (), s32[]{:S(2)}) async-start(), calls=%async_computation.11 | async-start | bytes 516096 | tf_op jit(solution)/shard_map/reduce_scatter | solution.py:35
  196.7 29.7 %all-to-all-start.6 = ((bf16[16,88,128]{2,1,0:T(8,128)(2,1)}), bf16[16,88,128]{2,1,0:T(8,128)(2,1)S(1)}, u32[]{:S(2)}, u32[]{:S(2)}) async-start(bf16[16,88,128]{2,1,0:T(8,128)(2,1)} %broadcast_in_dim.36), calls=%async_computation.7 | async-start | bytes 720896 | tf_op jit(solution)/shard_map/all_to_all | solution.py:22
  (9 other events, 14.3 us)
Sparse Core Ops, SparseCore 0:
  10.6 59.4 all-gather.1
  130.6 38.9 reduce-scatter.2
  186.4 39.9 reduce-scatter.4

commit v3 on v2

--- a/solution.py
+++ b/solution.py
@@ -40,7 +40,7 @@
     return jnp.concatenate([high, value - high], axis=-1).astype(jnp.bfloat16)
 
 
-def network_kernel(ring, weights, lcb, back, activ, d_pre):
+def network_kernel(ring, weights, lcb, back, mlp, activ, d_pre):
     f32, bf16 = jnp.float32, jnp.bfloat16
     split, end = F * K, weights.shape[1]
     cross = (((1,), (1,)), ((), ()))
@@ -53,15 +53,14 @@
     sigmoid = 1.0 / (1.0 + jnp.exp(-preact))
     activ[...] = (preact * sigmoid).astype(bf16)
     d_pre[...] = (d_hidden * sigmoid * (1.0 + preact * (1.0 - sigmoid))).astype(bf16)
-    back[:, :split] = jnp.dot(
-        d_pre[...], weights[:, :split], preferred_element_type=f32
-    ).astype(bf16)
-    for start in range(split, end, 512):
-        columns = slice(start, start + 512)
-        back[:, columns] = jnp.dot(
-            activ[...], weights[:, columns], preferred_element_type=f32
+    back[...] = jnp.dot(d_pre[...], weights[:, :split], preferred_element_type=f32).astype(bf16)
+    for start in range(0, end - split, 512):
+        mlp[:, start : start + 512] = jnp.dot(
+            activ[...],
+            weights[:, split + start : split + start + 512],
+            preferred_element_type=f32,
         ).astype(bf16)
-    back[:, end:] = lcb[...]
+    mlp[:, end - split :] = lcb[...]
 
 
 def network(ring, weights, lcb):
@@ -70,7 +69,8 @@
     return pl.pallas_call(
         network_kernel,
         out_shape=(
-            jax.ShapeDtypeStruct((samples, columns), jnp.bfloat16),
+            jax.ShapeDtypeStruct((samples, F * K), jnp.bfloat16),
+            jax.ShapeDtypeStruct((samples, columns - F * K), jnp.bfloat16),
             jax.ShapeDtypeStruct((samples, taps), jnp.bfloat16),
             jax.ShapeDtypeStruct((samples, taps), jnp.bfloat16),
         ),
@@ -135,10 +135,10 @@
 ):
     highest = lax.Precision.HIGHEST
     f32, bf16 = jnp.float32, jnp.bfloat16
-    shard, dp = ("x", "y"), ("z", "core")
+    shard, dp = ("x", "y"), ("zh", "zl", "core")
     far, near = lax.axis_size("x"), lax.axis_size("y")
-    depth, cores = lax.axis_size("z"), lax.axis_size("core")
-    members, groups = far * near, depth * cores
+    depth = lax.axis_size("zh") * lax.axis_size("zl")
+    members, groups = far * near, depth * lax.axis_size("core")
     batch = positions.shape[0]
     width = table.shape[1]
     rows_here = table.shape[0]
@@ -177,17 +177,19 @@
     lcb_part = jnp.einsum("bld,bfd->lf", grad_linear, embeds, preferred_element_type=f32)
     lcb_part = lcb_part.astype(bf16).reshape(near * batch, -1)
     spare = -lcb_part.shape[1] % LANES
-    back, activ, d_pre = network(ring, weights, jnp.pad(lcb_part, ((0, 0), (0, spare))))
-    back = exchange(back.reshape(near, batch, -1), "y")
+    lcb_padded = jnp.pad(lcb_part, ((0, 0), (0, spare)))
+    back, mlp_part, activ, d_pre = network(ring, weights, lcb_padded)
+    d_normed = exchange(back.reshape(near, batch, -1), "y")
     keep, send = weight_products(ring, activ, d_pre, hidden, depth)
     other = lax.ppermute(send, "core", [(0, 1), (1, 0)])
     weight_sum = (keep.astype(f32) + other.astype(f32)).astype(bf16).reshape(-1, hidden)
-    back, weight_sum = lax.optimization_barrier((back, weight_sum))
+    d_normed, mlp_part, _ = lax.optimization_barrier((d_normed, mlp_part, weight_sum))
     weight_sum = scatter(weight_sum, "x")
-    back = jnp.sum(back.astype(f32), axis=0)
-    split, end = F * K, F * K + NF * width
-    d_normed, mlp_out = back[:, :split], back[:, split:end]
-    lcb_mine = back[:, end : end + lcb_part.shape[1]].astype(bf16)
+    d_normed = jnp.sum(d_normed.astype(f32), axis=0)
+    mlp_sum = jnp.sum(exchange(mlp_part.reshape(near, batch, -1), "y").astype(f32), axis=0)
+    end = NF * width
+    mlp_out = mlp_sum[:, :end]
+    lcb_mine = mlp_sum[:, end : end + lcb_part.shape[1]].astype(bf16)
     d_linear = jnp.einsum("lf,bld->bfd", w_lcb, grad_linear, preferred_element_type=f32)
 
     gain_part = jnp.sum(d_normed * normal_part, axis=0)
@@ -209,6 +211,8 @@
     slot_grad = jnp.dot(slot_rows_hot, d_embeds, preferred_element_type=f32)
     slot_grad = slot_grad.reshape(members, CAP, width)
     slot_grad = jnp.where(live_mask[:, :, None], slot_grad, 0.0).astype(bf16)
+    slot_grad, weight_sum = lax.optimization_barrier((slot_grad, weight_sum))
+    weight_sum = scatter(weight_sum, "zh")
     proj_part = jnp.einsum("bfd,bdk->fk", embeds, halves(d_compressed), preferred_element_type=f32)
     proj_part = proj_part[:, :K] + proj_part[:, K:]
     small = jnp.concatenate([gain_part, proj_part.reshape(-1)]).astype(bf16).reshape(CAP, -1)
@@ -220,7 +224,7 @@
     lcb_sent = jnp.broadcast_to(lcb_mine[None], (members, *lcb_mine.shape))
     received = exchange(jnp.concatenate([sent, lcb_sent], axis=1), shard)
     received, weight_sum = lax.optimization_barrier((received, weight_sum))
-    weight_sum = scatter(weight_sum, "z")
+    weight_sum = scatter(weight_sum, "zl")
     returned = received[:, :CAP, :width].reshape(slots, width)
     small_end = width + 2 * F * K // CAP
     small = jnp.sum(received[:, :CAP, width:small_end].astype(f32), axis=0).astype(bf16)
@@ -238,8 +242,9 @@
     table_part = table_part.reshape(groups, -1, LANES)
     held = table_part.shape[1]
     total = exchange(jnp.concatenate([table_part, small], axis=1), dp)
-    total = spread(jnp.sum(total.astype(f32), axis=0).astype(bf16), dp)
+    total = jnp.sum(total.astype(f32), axis=0).astype(bf16)
     total, weight_sum = lax.optimization_barrier((total, weight_sum))
+    total = spread(total, dp)
     down_count = NF * width // groups
     grad_w_down = weight_sum[:down_count].T
     grad_w_up = weight_sum[down_count:]
@@ -258,9 +263,10 @@
 def solution(mesh):
     dp, shard = mesh.devices.shape
     near = min(8, shard // 2)
-    split = (dp // 2, 2, shard // near, near)
-    mesh = jax.sharding.Mesh(mesh.devices.reshape(split), ("z", "core", "x", "y"))
-    dp, shard = ("z", "core"), ("x", "y")
+    low = 2 if dp % 4 == 0 else 1
+    split = (dp // 2 // low, low, 2, shard // near, near)
+    dp, shard = ("zh", "zl", "core"), ("x", "y")
+    mesh = jax.sharding.Mesh(mesh.devices.reshape(split), (*dp, *shard))
     every = (*dp, *shard)
     placed = (
         P(shard, None),

time: 240 us -> 257 us (1.071)
  the two profiles are of different devices: /device:TPU:8 before, /device:TPU:1 now
where the time goes in v3:
time: 257 us; the launch traced here: 256 us
  waiting for transfers between devices  127 us (49%)
  starting transfers between devices  40.9 us (16%)
  matrix products  20 us (8%)
  blocking collectives  18.9 us (7%)
  local copies, waits for them, and re-layouts  16.5 us (6%)
  between operations  14.3 us (6%)
  other arithmetic  12.7 us (5%)
  Pallas kernels  5.6 us (2%)
    all_to_all x7, waiting for transfers between devices, exchange(): return lax.all_to_all(blocks, axis, split_axis=0, concat_axis=0, tiled=True)  77.1 us
    reduce_scatter x3, waiting for transfers between devices, scatter(): return lax.psum_scatter(blocks, axis, scatter_dimension=0, tiled=True)  44.9 us
    all_to_all x7, starting transfers between devices, exchange(): return lax.all_to_all(blocks, axis, split_axis=0, concat_axis=0, tiled=True)  34.9 us
    all_to_all x1, blocking collectives, exchange(): return lax.all_to_all(blocks, axis, split_axis=0, concat_axis=0, tiled=True)  18.9 us
    ppermute x1, starting transfers between devices, body(): other = lax.ppermute(send, 'core', [(0, 1), (1, 0)])  5.91 us
  transfers between devices with their start and end apart: 12, of which 9 were waited for; matrix products, arithmetic and copies ran while one was open for 14% of the time, Pallas kernels for 0%

profile of v3, /device:TPU:1, one launch (start us, length us, event | category | flops | bytes accessed | tf_op | source)
XLA Modules:
  0.0 255.6 jit_solution(17825116054127559937)
XLA Ops:
  8.4 2.1 pad_maximum_fusion
  10.5 18.9 %all_to_all.44 = s32[32,1,32]{2,1,0:T(1,128)S(1)} all-to-all(s32[32,1,32]{2,1,0:T(1,128)S(1)} %bitcast.134), channel_id=1, replica_groups=mesh['zh'=4,'zl'=2,'core'=2,'x'=4,'y'=8] {'x','y'}, dimensions={0} | all-to-all | bytes 8192 | tf_op jit(solution)/shard_map/all_to_all | solution.py:22
  32.8 4.0 %all-to-all-start.1 = ((bf16[32,32,160]{2,1,0:T(8,128)(2,1)}), bf16[32,32,160]{2,1,0:T(8,128)(2,1)S(1)}, u32[]{:S(2)}, u32[]{:S(2)}) async-start(bf16[32,32,160]{2,1,0:T(8,128)(2,1)} %bitcast.3), calls=%async_computation.1 | async-start | bytes 1048576 | tf_op jit(solution)/shard_map/all_to_all | solution.py:22
  37.4 12.4 %all-to-all-done.1 = bf16[32,32,160]{2,1,0:T(8,128)(2,1)S(1)} async-done(((bf16[32,32,160]{2,1,0:T(8,128)(2,1)}), bf16[32,32,160]{2,1,0:T(8,128)(2,1)S(1)}, u32[]{:S(2)}, u32[]{:S(2)}) %all-to-all-start.1) | async-done | bytes 327712 | tf_op jit(solution)/shard_map/all_to_all | solution.py:22
  50.0 2.3 fusion.8
  57.1 5.5 %all-to-all-start.2 = ((bf16[8,16,3584]{2,1,0:T(8,128)(2,1)}), bf16[8,16,3584]{2,1,0:T(8,128)(2,1)S(1)}, u32[]{:S(2)}, u32[]{:S(2)}) async-start(bf16[8,16,3584]{2,1,0:T(8,128)(2,1)} %broadcast_in_dim.32), calls=%async_computation.2 | async-start | bytes 1835008 | tf_op jit(solution)/shard_map/all_to_all | solution.py:22
  65.4 20.1 %all-to-all-done.2 = bf16[8,16,3584]{2,1,0:T(8,128)(2,1)S(1)} async-done(((bf16[8,16,3584]{2,1,0:T(8,128)(2,1)}), bf16[8,16,3584]{2,1,0:T(8,128)(2,1)S(1)}, u32[]{:S(2)}, u32[]{:S(2)}) %all-to-all-start.2) | async-done | bytes 917536 | tf_op jit(solution)/shard_map/all_to_all | solution.py:22
  87.5 2.8 %shard_map.153 = (bf16[128,1024]{1,0:T(8,128)(2,1)}, bf16[128,2688]{1,0:T(8,128)(2,1)}, bf16[128,512]{1,0:T(8,128)(2,1)S(1)}, bf16[128,512]{1,0:T(8,128)(2,1)S(1)}) custom-call(bf16[128,3584]{1,0:T(8,128)(2,1)S(1)} %bitcast.117, bf16[512,3584]{1,0:T(8,128)(2,1)S(1)} %copy-done.1, bf16[128,128]{1,0:T(8,128)(2,1)S(1)} %pad.12.lcb), custom_call_target="tpu_custom_call" | custom-call | flops 973078528 | bytes 6000000 | tf_op jit(solution)/shard_map/pallas_call | solution.py:69
  90.3 2.8 %shard_map.154 = (bf16[4,8,224,128]{3,2,1,0:T(8,128)(2,1)S(1)}, bf16[4,8,224,128]{3,2,1,0:T(8,128)(2,1)S(1)}) custom-call(s32[1]{0:T(128)} %bitcast.12.me, bf16[128,3584]{1,0:T(8,128)(2,1)S(1)} %bitcast.118, bf16[128,512]{1,0:T(8,128)(2,1)S(1)} %get-tuple-element.23.activ, bf16[128,512]{1,0:T(8,128)(2,1)S(1)} %get-tuple-element.24.d_pre), custom_call_target="tpu_custom_call" | custom-call | flops 469762048 | bytes 6000000 | tf_op jit(solution)/shard_map/pallas_call | solution.py:113
  93.1 5.9 %collective-permute-start = (bf16[4,8,224,128]{3,2,1,0:T(8,128)(2,1)S(1)}, bf16[4,8,224,128]{3,2,1,0:T(8,128)(2,1)S(1)}, u32[]{:S(2)}, u32[]{:S(2)}) collective-permute-start(bf16[4,8,224,128]{3,2,1,0:T(8,128)(2,1)S(1)} %get-tuple-element.26), channel_id=1, source_target_pairs={{0,32},{32,0},{1,33},{33,1},{2,34},{34,2},{3,35},{35,3},{4,36},{36... | collective-permute-start | bytes 5505032 | tf_op jit(solution)/shard_map/ppermute | solution.py:184
  99.1 3.4 %collective-permute-done = bf16[4,8,224,128]{3,2,1,0:T(8,128)(2,1)S(1)} collective-permute-done((bf16[4,8,224,128]{3,2,1,0:T(8,128)(2,1)S(1)}, bf16[4,8,224,128]{3,2,1,0:T(8,128)(2,1)S(1)}, u32[]{:S(2)}, u32[]{:S(2)}) %collective-permute-start) | collective-permute-done | bytes 1835040 | tf_op jit(solution)/shard_map/ppermute | solution.py:184
  104.2 3.6 %all-to-all-start.3 = ((bf16[8,16,1024]{2,1,0:T(8,128)(2,1)}), bf16[8,16,1024]{2,1,0:T(8,128)(2,1)S(1)}, u32[]{:S(2)}, u32[]{:S(2)}) async-start(bf16[8,16,1024]{2,1,0:T(8,128)(2,1)} %bitcast.11), calls=%async_computation.3 | async-start | bytes 524288 | tf_op jit(solution)/shard_map/all_to_all | solution.py:22
  109.5 10.0 %all-to-all-done.3 = bf16[8,16,1024]{2,1,0:T(8,128)(2,1)S(1)} async-done(((bf16[8,16,1024]{2,1,0:T(8,128)(2,1)}), bf16[8,16,1024]{2,1,0:T(8,128)(2,1)S(1)}, u32[]{:S(2)}, u32[]{:S(2)}) %all-to-all-start.3) | async-done | bytes 262176 | tf_op jit(solution)/shard_map/all_to_all | solution.py:22
  123.6 4.3 %all-to-all-start.4 = ((bf16[8,16,2688]{2,1,0:T(8,128)(2,1)}), bf16[8,16,2688]{2,1,0:T(8,128)(2,1)}, u32[]{:S(2)}, u32[]{:S(2)}) async-start(bf16[8,16,2688]{2,1,0:T(8,128)(2,1)} %bitcast.14), calls=%async_computation.4 | async-start | bytes 1376256 | tf_op jit(solution)/shard_map/all_to_all | solution.py:22
  131.3 2.4 fusion.13
  136.0 13.4 %all-to-all-done.4 = bf16[8,16,2688]{2,1,0:T(8,128)(2,1)} async-done(((bf16[8,16,2688]{2,1,0:T(8,128)(2,1)}), bf16[8,16,2688]{2,1,0:T(8,128)(2,1)}, u32[]{:S(2)}, u32[]{:S(2)}) %all-to-all-start.4) | async-done | bytes 688160 | tf_op jit(solution)/shard_map/all_to_all | solution.py:22
  151.7 3.9 %all-to-all-start.5 = ((bf16[32,40,256]{2,1,0:T(8,128)(2,1)}), bf16[32,40,256]{2,1,0:T(8,128)(2,1)S(1)}, u32[]{:S(2)}, u32[]{:S(2)}) async-start(bf16[32,40,256]{2,1,0:T(8,128)(2,1)} %pad_maximum_fusion.1), calls=%async_computation.6 | async-start | bytes 1310720 | tf_op jit(solution)/shard_map/all_to_all | solution.py:22
  156.4 36.1 %reduce-scatter.6.cloned.1.call-done = bf16[448,128]{1,0:T(8,128)(2,1)} async-done(((bf16[1792,128]{1,0:T(8,128)(2,1)}), bf16[448,128]{1,0:T(8,128)(2,1)}) %reduce-scatter.6.cloned.1.call-update) | async-done | bytes 114704 | tf_op jit(solution)/shard_map/reduce_scatter | solution.py:35
  194.9 6.3 %all-to-all-start.6 = ((bf16[16,88,128]{2,1,0:T(8,128)(2,1)}), bf16[16,88,128]{2,1,0:T(8,128)(2,1)S(1)}, u32[]{:S(2)}, u32[]{:S(2)}) async-start(bf16[16,88,128]{2,1,0:T(8,128)(2,1)} %pad_maximum_fusion.2), calls=%async_computation.8 | async-start | bytes 720896 | tf_op jit(solution)/shard_map/all_to_all | solution.py:22
  201.7 13.3 %all-to-all-done.6 = bf16[16,88,128]{2,1,0:T(8,128)(2,1)S(1)} async-done(((bf16[16,88,128]{2,1,0:T(8,128)(2,1)}), bf16[16,88,128]{2,1,0:T(8,128)(2,1)S(1)}, u32[]{:S(2)}, u32[]{:S(2)}) %all-to-all-start.6) | async-done | bytes 360480 | tf_op jit(solution)/shard_map/all_to_all | solution.py:22
  215.0 8.8 %reduce-scatter.8.cloned.1.call-done = bf16[224,128]{1,0:T(8,128)(2,1)} async-done(((bf16[448,128]{1,0:T(8,128)(2,1)}), bf16[224,128]{1,0:T(8,128)(2,1)}) %reduce-scatter.8.cloned.1.call-update) | async-done | bytes 57360 | tf_op jit(solution)/shard_map/reduce_scatter | solution.py:35
  224.6 7.3 %all-to-all-start.7 = ((bf16[16,88,128]{2,1,0:T(8,128)(2,1)}), bf16[16,88,128]{2,1,0:T(8,128)(2,1)S(1)}, u32[]{:S(2)}, u32[]{:S(2)}) async-start(bf16[16,88,128]{2,1,0:T(8,128)(2,1)} %broadcast_in_dim.36), calls=%async_computation.10 | async-start | bytes 720896 | tf_op jit(solution)/shard_map/all_to_all | solution.py:22
  233.8 2.6 %fusion.14 = bf16[16,128,160]{1,2,0:T(8,128)(2,1)} fusion(f32[16,112,160]{1,2,0:T(8,128)} %convolution_bitcast_fusion.2, f32[16,16,160]{1,2,0:T(8,128)S(1)} %copy.58, bf16[2048,160]{0,1:T(8,128)(2,1)S(1)} %fusion.8), kind=kLoop, calls=%fused_computation.24 | loop fusion | flops 1310720 | bytes 2621440 | tf_op jit(solution)/shard_map/convert_element_type | solution.py:259
  237.6 8.0 %all-to-all-done.7 = bf16[16,88,128]{2,1,0:T(8,128)(2,1)S(1)} async-done(((bf16[16,88,128]{2,1,0:T(8,128)(2,1)}), bf16[16,88,128]{2,1,0:T(8,128)(2,1)S(1)}, u32[]{:S(2)}, u32[]{:S(2)}) %all-to-all-start.7) | async-done | bytes 360480 | tf_op jit(solution)/shard_map/all_to_all | solution.py:22
  (120 shorter events, 41.2 us)
Async XLA Ops:
  7.2 23.5 %copy-start = (bf16[1024,160]{0,1:T(8,128)(2,1)S(1)}, bf16[1024,160]{0,1:T(8,128)(2,1)}, u32[]{:S(2)}) copy-start(bf16[1024,160]{0,1:T(8,128)(2,1)} %param.10) | copy-start | bytes 983044
  7.2 78.3 %all-gather.2.cloned.1.call-start = ((), (), s32[]{:S(2)}) async-start(), calls=%async_computation.11 | async-start | bytes 4587520 | tf_op jit(solution)/shard_map/all_gather | solution.py:31
  8.4 2.1 copy-start.8
  31.8 5.1 %copy-start.2 = (bf16[16,128,160]{1,2,0:T(8,128)(2,1)S(1)}, bf16[16,128,160]{1,2,0:T(8,128)(2,1)}, u32[]{:S(2)}) copy-start(bf16[16,128,160]{1,2,0:T(8,128)(2,1)} %param.19) | copy-start | bytes 1966084
  31.8 5.6 %copy-start.10 = (s32[1,1,32]{2,1,0:T(1,128)S(1)}, s32[1,1,32]{2,1,0:T(1,128)}, u32[]{:S(2)}) copy-start(s32[1,1,32]{2,1,0:T(1,128)} %param.12) | copy-start | bytes 388
  32.8 17.2 %copy-start.11 = (s32[16,128]{1,0:T(8,128)S(1)}, s32[16,128]{1,0:T(8,128)}, u32[]{:S(2)}) copy-start(s32[16,128]{1,0:T(8,128)} %param.13) | copy-start | bytes 24580
  32.8 17.0 %all-to-all-start.1 = ((bf16[32,32,160]{2,1,0:T(8,128)(2,1)}), bf16[32,32,160]{2,1,0:T(8,128)(2,1)S(1)}, u32[]{:S(2)}, u32[]{:S(2)}) async-start(bf16[32,32,160]{2,1,0:T(8,128)(2,1)} %bitcast.3), calls=%async_computation.1 | async-start | bytes 1048576 | tf_op jit(solution)/shard_map/all_to_all | solution.py:22
  50.0 2.5 copy-start.9
  54.1 1.8 copy-start.7
  57.1 28.4 %all-to-all-start.2 = ((bf16[8,16,3584]{2,1,0:T(8,128)(2,1)}), bf16[8,16,3584]{2,1,0:T(8,128)(2,1)S(1)}, u32[]{:S(2)}, u32[]{:S(2)}) async-start(bf16[8,16,3584]{2,1,0:T(8,128)(2,1)} %broadcast_in_dim.32), calls=%async_computation.2 | async-start | bytes 1835008 | tf_op jit(solution)/shard_map/all_to_all | solution.py:22
  62.6 88.2 %reduce-scatter.4.cloned.1.call-start = ((), (), s32[]{:S(2)}) async-start(), calls=%async_computation.12 | async-start | bytes 2293760 | tf_op jit(solution)/shard_map/reduce_scatter | solution.py:35
  85.5 2.0 copy-start.1
  93.1 9.3 %collective-permute-start = (bf16[4,8,224,128]{3,2,1,0:T(8,128)(2,1)S(1)}, bf16[4,8,224,128]{3,2,1,0:T(8,128)(2,1)S(1)}, u32[]{:S(2)}, u32[]{:S(2)}) collective-permute-start(bf16[4,8,224,128]{3,2,1,0:T(8,128)(2,1)S(1)} %get-tuple-element.26), channel_id=1, source_target_pairs={{0,32},{32,0},{1,33},{33,1},{2,34},{34,2},{3,35},{35,3},{4,36},{36... | collective-permute-start | bytes 5505032 | tf_op jit(solution)/shard_map/ppermute | solution.py:184
  104.2 3.8 %copy-start.5 = (bf16[112,128]{1,0:T(8,128)(2,1)S(1)}, bf16[112,128]{1,0:T(8,128)(2,1)}, u32[]{:S(2)}) copy-start(bf16[112,128]{1,0:T(8,128)(2,1)} %param.18) | copy-start | bytes 86020
  104.2 15.3 %all-to-all-start.3 = ((bf16[8,16,1024]{2,1,0:T(8,128)(2,1)}), bf16[8,16,1024]{2,1,0:T(8,128)(2,1)S(1)}, u32[]{:S(2)}, u32[]{:S(2)}) async-start(bf16[8,16,1024]{2,1,0:T(8,128)(2,1)} %bitcast.11), calls=%async_computation.3 | async-start | bytes 524288 | tf_op jit(solution)/shard_map/all_to_all | solution.py:22
  123.6 6.5 %copy-start.4 = (f32[16,160,8]{1,2,0:T(8,128)S(1)}, f32[16,160,8]{1,2,0:T(8,128)}, u32[]{:S(2)}) copy-start(f32[16,160,8]{1,2,0:T(8,128)} %get-tuple-element.57) | copy-start | bytes 245764
  123.6 25.8 %all-to-all-start.4 = ((bf16[8,16,2688]{2,1,0:T(8,128)(2,1)}), bf16[8,16,2688]{2,1,0:T(8,128)(2,1)}, u32[]{:S(2)}, u32[]{:S(2)}) async-start(bf16[8,16,2688]{2,1,0:T(8,128)(2,1)} %bitcast.14), calls=%async_computation.4 | async-start | bytes 1376256 | tf_op jit(solution)/shard_map/all_to_all | solution.py:22
  127.9 3.4 %copy-start.3 = (f32[16,128,160]{1,2,0:T(8,128)S(1)}, f32[16,128,160]{1,2,0:T(8,128)}, u32[]{:S(2)}) copy-start(f32[16,128,160]{1,2,0:T(8,128)} %fusion.12) | copy-start | bytes 3932164
  151.7 40.8 %all-to-all-start.5 = ((bf16[32,40,256]{2,1,0:T(8,128)(2,1)}), bf16[32,40,256]{2,1,0:T(8,128)(2,1)S(1)}, u32[]{:S(2)}, u32[]{:S(2)}) async-start(bf16[32,40,256]{2,1,0:T(8,128)(2,1)} %pad_maximum_fusion.1), calls=%async_computation.6 | async-start | bytes 1310720 | tf_op jit(solution)/shard_map/all_to_all | solution.py:22
  155.7 36.9 %reduce-scatter.6.cloned.1.call-start = ((), (), s32[]{:S(2)}) async-start(), calls=%async_computation.13 | async-start | bytes 573440 | tf_op jit(solution)/shard_map/reduce_scatter | solution.py:35
  194.9 20.1 %all-to-all-start.6 = ((bf16[16,88,128]{2,1,0:T(8,128)(2,1)}), bf16[16,88,128]{2,1,0:T(8,128)(2,1)S(1)}, u32[]{:S(2)}, u32[]{:S(2)}) async-start(bf16[16,88,128]{2,1,0:T(8,128)(2,1)} %pad_maximum_fusion.2), calls=%async_computation.8 | async-start | bytes 720896 | tf_op jit(solution)/shard_map/all_to_all | solution.py:22
  201.1 22.6 %reduce-scatter.8.cloned.1.call-start = ((), (), s32[]{:S(2)}) async-start(), calls=%async_computation.14 | async-start | bytes 172032 | tf_op jit(solution)/shard_map/reduce_scatter | solution.py:35
  224.6 21.1 %all-to-all-start.7 = ((bf16[16,88,128]{2,1,0:T(8,128)(2,1)}), bf16[16,88,128]{2,1,0:T(8,128)(2,1)S(1)}, u32[]{:S(2)}, u32[]{:S(2)}) async-start(bf16[16,88,128]{2,1,0:T(8,128)(2,1)} %broadcast_in_dim.36), calls=%async_computation.10 | async-start | bytes 720896 | tf_op jit(solution)/shard_map/all_to_all | solution.py:22
  233.8 2.6 %copy-start.6 = (bf16[224,128]{1,0:T(8,128)(2,1)S(1)}, bf16[224,128]{1,0:T(8,128)(2,1)}, u32[]{:S(2)}) copy-start(bf16[224,128]{1,0:T(8,128)(2,1)} %reduce-scatter.8.cloned.1.call-done) | copy-start | bytes 172036
Sparse Core Ops, SparseCore 0:
  10.6 60.3 all-gather.1
  104.3 31.9 reduce-scatter.3
  159.3 33.1 reduce-scatter.5
  204.6 19.1 reduce-scatter.7

commit v4 on v2

--- a/solution.py
+++ b/solution.py
@@ -1,3 +1,5 @@
+import functools
+
 import jax
 import jax.numpy as jnp
 from jax import lax
@@ -40,9 +42,17 @@
     return jnp.concatenate([high, value - high], axis=-1).astype(jnp.bfloat16)
 
 
-def network_kernel(ring, weights, lcb, back, activ, d_pre):
+def halved(blocks, axis, step):
+    half = blocks.shape[0] // 2
+    pairs = [(i, i ^ step) for i in range(lax.axis_size(axis))]
+    other = lax.ppermute(blocks[half:], axis, pairs)
+    return (blocks[:half].astype(jnp.float32) + other.astype(jnp.float32)).astype(jnp.bfloat16)
+
+
+def network_kernel(batch, me, ring, weights, lcb, back, mlp, mine, shuffled):
     f32, bf16 = jnp.float32, jnp.bfloat16
-    split, end = F * K, weights.shape[1]
+    samples, columns = ring.shape
+    split, taps = F * K, weights.shape[0]
     cross = (((1,), (1,)), ((), ()))
     preact = lax.dot_general(
         ring[:, :split], weights[:, :split], cross, preferred_element_type=f32
@@ -51,83 +61,87 @@
         ring[:, split:], weights[:, split:], cross, preferred_element_type=f32
     )
     sigmoid = 1.0 / (1.0 + jnp.exp(-preact))
-    activ[...] = (preact * sigmoid).astype(bf16)
-    d_pre[...] = (d_hidden * sigmoid * (1.0 + preact * (1.0 - sigmoid))).astype(bf16)
-    back[:, :split] = jnp.dot(
-        d_pre[...], weights[:, :split], preferred_element_type=f32
-    ).astype(bf16)
-    for start in range(split, end, 512):
-        columns = slice(start, start + 512)
-        back[:, columns] = jnp.dot(
-            activ[...], weights[:, columns], preferred_element_type=f32
+    activ = (preact * sigmoid).astype(bf16)
+    d_pre = (d_hidden * sigmoid * (1.0 + preact * (1.0 - sigmoid))).astype(bf16)
+    mine[:, :columns] = ring[...]
+    mine[:, columns : columns + taps] = activ
+    mine[:, columns + taps :] = d_pre
+    back[:, :split] = jnp.dot(d_pre, weights[:, :split], preferred_element_type=f32).astype(bf16)
+    back[:, split:] = lcb[...]
+    for block in range(samples // batch):
+        start = pl.multiple_of((me[0] ^ block) * batch, batch)
+        shuffled[pl.ds(start, batch), :] = activ[block * batch : (block + 1) * batch]
+    for start in range(0, columns - split, 512):
+        mlp[:, start : start + 512] = jnp.dot(
+            shuffled[...],
+            weights[:, split + start : split + start + 512],
+            preferred_element_type=f32,
         ).astype(bf16)
-    back[:, end:] = lcb[...]
-
-
-def network(ring, weights, lcb):
-    samples, taps = ring.shape[0], weights.shape[0]
-    columns = weights.shape[1] + lcb.shape[1]
+
+
+def network(ring, weights, lcb, batch):
+    samples, columns = ring.shape
+    taps = weights.shape[0]
+    vmem = pl.BlockSpec(memory_space=pltpu.VMEM)
+    shape = lambda width: jax.ShapeDtypeStruct((samples, width), jnp.bfloat16)
     return pl.pallas_call(
-        network_kernel,
-        out_shape=(
-            jax.ShapeDtypeStruct((samples, columns), jnp.bfloat16),
-            jax.ShapeDtypeStruct((samples, taps), jnp.bfloat16),
-            jax.ShapeDtypeStruct((samples, taps), jnp.bfloat16),
-        ),
+        functools.partial(network_kernel, batch),
+        in_specs=[pl.BlockSpec(memory_space=pltpu.SMEM), vmem, vmem, vmem],
+        out_shape=(shape(F * K + lcb.shape[1]), shape(columns - F * K), shape(columns + 2 * taps)),
+        scratch_shapes=[pltpu.VMEM((samples, taps), jnp.bfloat16)],
         compiler_params=pltpu.CompilerParams(vmem_limit_bytes=32 * 2**20),
         cost_estimate=pl.CostEstimate(
-            flops=4 * samples * taps * columns, bytes_accessed=6_000_000, transcendentals=65536
+            flops=4 * samples * taps * columns, bytes_accessed=7_000_000, transcendentals=65536
         ),
-    )(ring, weights, lcb)
-
-
-def weight_kernel(me, ring, activ, d_pre, keep, send):
-    _, depth, _, _ = keep.shape
+    )(lax.axis_index("y").reshape(1), ring, weights, lcb)
+
+
+def weight_kernel(me, mine, other, activ, activ_other, d_pre, d_pre_other, out):
+    _, depth, _, _ = out.shape
+    f32 = jnp.float32
+    along = (((0,), (0,)), ((), ()))
     first = me[0] == 0
-    split = F * K
+    split, columns = F * K, mine.shape[1]
     start = 0
-    for begin, end, right in ((split, ring.shape[1], activ), (0, split, d_pre)):
+    for begin, end, right, right_other in (
+        (split, columns, activ, activ_other),
+        (0, split, d_pre, d_pre_other),
+    ):
         rows = (end - begin) // (2 * depth)
         for z in range(depth):
-            at = begin + z * 2 * rows
-            part = lax.dot_general(
-                ring[:, at : at + 2 * rows],
-                right[...],
-                (((0,), (0,)), ((), ())),
-                preferred_element_type=jnp.float32,
+            at = slice(begin + z * 2 * rows, begin + (z + 1) * 2 * rows)
+            part = lax.dot_general(mine[:, at], right[...], along, preferred_element_type=f32)
+            part = part + lax.dot_general(
+                other[:, at], right_other[...], along, preferred_element_type=f32
             )
-            low, high = part[:rows], part[rows:]
-            here = slice(start, start + rows)
-            keep[0, z, here] = jnp.where(first, low, high).astype(jnp.bfloat16)
-            send[0, z, here] = jnp.where(first, high, low).astype(jnp.bfloat16)
+            part = jnp.where(first, part[:rows], part[rows:])
+            out[0, z, start : start + rows] = part.astype(jnp.bfloat16)
         start += rows
 
 
-def weight_products(ring, activ, d_pre, hidden, depth):
-    samples = ring.shape[0]
-    far = activ.shape[1] // hidden
-    rows = ring.shape[1] // (2 * depth)
-    chunk = pl.BlockSpec((samples, hidden), lambda j: (0, j))
-    half = pl.BlockSpec((1, depth, rows, hidden), lambda j: (j, 0, 0, 0))
-    shape = jax.ShapeDtypeStruct((far, depth, rows, hidden), jnp.bfloat16)
+def weight_products(mine, other, hidden, far, depth):
+    samples = mine.shape[0]
+    columns = mine.shape[1] - 2 * far * hidden
+    rows = columns // (2 * depth)
+    first = columns // hidden
+    ring = pl.BlockSpec((samples, columns), lambda j: (0, 0))
+    activ = pl.BlockSpec((samples, hidden), lambda j: (0, first + j))
+    d_pre = pl.BlockSpec((samples, hidden), lambda j: (0, first + far + j))
     return pl.pallas_call(
         weight_kernel,
         grid=(far,),
         in_specs=[
-            pl.BlockSpec(memory_space=pltpu.SMEM),
-            pl.BlockSpec(ring.shape, lambda j: (0, 0)),
-            chunk,
-            chunk,
+            pl.BlockSpec(memory_space=pltpu.SMEM), ring, ring, activ, activ, d_pre, d_pre
         ],
-        out_specs=(half, half),
-        out_shape=(shape, shape),
+        out_specs=pl.BlockSpec((1, depth, rows, hidden), lambda j: (j, 0, 0, 0)),
+        out_shape=jax.ShapeDtypeStruct((far, depth, rows, hidden), jnp.bfloat16),
         compiler_params=pltpu.CompilerParams(vmem_limit_bytes=32 * 2**20),
         cost_estimate=pl.CostEstimate(
-            flops=4 * samples * rows * depth * far * hidden,
+            flops=8 * samples * rows * depth * far * hidden,
             bytes_accessed=6_000_000,
             transcendentals=0,
         ),
-    )(lax.axis_index("core").reshape(1), ring, activ, d_pre)
+    )(lax.axis_index("core").reshape(1), mine, other, mine, other, mine, other)
 
 
 def body(
@@ -137,8 +151,8 @@
     f32, bf16 = jnp.float32, jnp.bfloat16
     shard, dp = ("x", "y"), ("z", "core")
     far, near = lax.axis_size("x"), lax.axis_size("y")
-    depth, cores = lax.axis_size("z"), lax.axis_size("core")
-    members, groups = far * near, depth * cores
+    depth = lax.axis_size("z")
+    members, groups = far * near, depth * lax.axis_size("core")
     batch = positions.shape[0]
     width = table.shape[1]
     rows_here = table.shape[0]
@@ -177,17 +191,16 @@
     lcb_part = jnp.einsum("bld,bfd->lf", grad_linear, embeds, preferred_element_type=f32)
     lcb_part = lcb_part.astype(bf16).reshape(near * batch, -1)
     spare = -lcb_part.shape[1] % LANES
-    back, activ, d_pre = network(ring, weights, jnp.pad(lcb_part, ((0, 0), (0, spare))))
+    lcb_padded = jnp.pad(lcb_part, ((0, 0), (0, spare)))
+    back, mlp_part, mine = network(ring, weights, lcb_padded, batch)
     back = exchange(back.reshape(near, batch, -1), "y")
-    keep, send = weight_products(ring, activ, d_pre, hidden, depth)
-    other = lax.ppermute(send, "core", [(0, 1), (1, 0)])
-    weight_sum = (keep.astype(f32) + other.astype(f32)).astype(bf16).reshape(-1, hidden)
-    back, weight_sum = lax.optimization_barrier((back, weight_sum))
+    other = lax.ppermute(mine, "core", [(0, 1), (1, 0)])
+    weight_sum = weight_products(mine, other, hidden, far, depth).reshape(-1, hidden)
+    back, _ = lax.optimization_barrier((back, weight_sum))
     weight_sum = scatter(weight_sum, "x")
     back = jnp.sum(back.astype(f32), axis=0)
-    split, end = F * K, F * K + NF * width
-    d_normed, mlp_out = back[:, :split], back[:, split:end]
-    lcb_mine = back[:, end : end + lcb_part.shape[1]].astype(bf16)
+    d_normed = back[:, : F * K]
+    lcb_mine = back[:, F * K : F * K + lcb_part.shape[1]].astype(bf16)
     d_linear = jnp.einsum("lf,bld->bfd", w_lcb, grad_linear, preferred_element_type=f32)
 
     gain_part = jnp.sum(d_normed * normal_part, axis=0)
@@ -209,6 +222,13 @@
     slot_grad = jnp.dot(slot_rows_hot, d_embeds, preferred_element_type=f32)
     slot_grad = slot_grad.reshape(members, CAP, width)
     slot_grad = jnp.where(live_mask[:, :, None], slot_grad, 0.0).astype(bf16)
+    slot_grad, mlp_part = lax.optimization_barrier((slot_grad, mlp_part))
+    mlp_part = halved(mlp_part, "y", near // 2)
+    step = near // 4
+    while step:
+        mlp_part = halved(mlp_part, "y", step)
+        step //= 2
+    mlp_out = mlp_part.astype(f32)
     proj_part = jnp.einsum("bfd,bdk->fk", embeds, halves(d_compressed), preferred_element_type=f32)
     proj_part = proj_part[:, :K] + proj_part[:, K:]
     small = jnp.concatenate([gain_part, proj_part.reshape(-1)]).astype(bf16).reshape(CAP, -1)
@@ -238,7 +258,9 @@
     table_part = table_part.reshape(groups, -1, LANES)
     held = table_part.shape[1]
     total = exchange(jnp.concatenate([table_part, small], axis=1), dp)
-    total = spread(jnp.sum(total.astype(f32), axis=0).astype(bf16), dp)
+    total = jnp.sum(total.astype(f32), axis=0).astype(bf16)
+    total, mlp_out = lax.optimization_barrier((total, mlp_out))
+    total = spread(total, dp)
     total, weight_sum = lax.optimization_barrier((total, weight_sum))
     down_count = NF * width // groups
     grad_w_down = weight_sum[:down_count].T
@@ -259,8 +281,8 @@
     dp, shard = mesh.devices.shape
     near = min(8, shard // 2)
     split = (dp // 2, 2, shard // near, near)
-    mesh = jax.sharding.Mesh(mesh.devices.reshape(split), ("z", "core", "x", "y"))
     dp, shard = ("z", "core"), ("x", "y")
+    mesh = jax.sharding.Mesh(mesh.devices.reshape(split), (*dp, *shard))
     every = (*dp, *shard)
     placed = (
         P(shard, None),

time: 240 us -> 241 us (level)
  the two profiles are of different devices: /device:TPU:8 before, /device:TPU:1 now
where the time goes in v4:
time: 241 us; the launch traced here: 236 us
  waiting for transfers between devices  93.3 us (39%)
  starting transfers between devices  48.7 us (20%)
  local copies, waits for them, and re-layouts  20.5 us (9%)
  matrix products  20 us (8%)
  blocking collectives  18.9 us (8%)
  between operations  14.4 us (6%)
  other arithmetic  12.8 us (5%)
  Pallas kernels  7.37 us (3%)
    all_to_all x6, waiting for transfers between devices, exchange(): return lax.all_to_all(blocks, axis, split_axis=0, concat_axis=0, tiled=True)  48.3 us
    all_to_all x6, starting transfers between devices, exchange(): return lax.all_to_all(blocks, axis, split_axis=0, concat_axis=0, tiled=True)  34.2 us
    ppermute x3, waiting for transfers between devices, halved(): other = lax.ppermute(blocks[half:], axis, pairs)  27 us
    all_to_all x1, blocking collectives, exchange(): return lax.all_to_all(blocks, axis, split_axis=0, concat_axis=0, tiled=True)  18.9 us
    reduce_scatter x2, waiting for transfers between devices, scatter(): return lax.psum_scatter(blocks, axis, scatter_dimension=0, tiled=True)  17.2 us
    ppermute x3, starting transfers between devices, halved(): other = lax.ppermute(blocks[half:], axis, pairs)  8.24 us
    unnamed x52, local copies, waits for them, and re-layouts  7.7 us
    ppermute x1, starting transfers between devices, body(): other = lax.ppermute(mine, 'core', [(0, 1), (1, 0)])  5.9 us
  transfers between devices with their start and end apart: 13, of which 7 were waited for; matrix products, arithmetic and copies ran while one was open for 17% of the time, Pallas kernels for 2%

profile of v4, /device:TPU:1, one launch (start us, length us, event | category | flops | bytes accessed | tf_op | source)
XLA Modules:
  0.0 235.9 jit_solution(1120738509963647525)
XLA Ops:
  8.4 2.1 pad_maximum_fusion
  10.5 18.9 %all_to_all.39 = s32[32,1,32]{2,1,0:T(1,128)S(1)} all-to-all(s32[32,1,32]{2,1,0:T(1,128)S(1)} %bitcast.132), channel_id=1, replica_groups=mesh['z'=8,'core'=2,'x'=4,'y'=8] {'x','y'}, dimensions={0} | all-to-all | bytes 8192 | tf_op jit(solution)/shard_map/all_to_all | solution.py:24
  32.8 4.0 %all-to-all-start.1 = ((bf16[32,32,160]{2,1,0:T(8,128)(2,1)}), bf16[32,32,160]{2,1,0:T(8,128)(2,1)S(1)}, u32[]{:S(2)}, u32[]{:S(2)}) async-start(bf16[32,32,160]{2,1,0:T(8,128)(2,1)} %bitcast.3), calls=%async_computation.1 | async-start | bytes 1048576 | tf_op jit(solution)/shard_map/all_to_all | solution.py:24
  37.5 12.4 %all-to-all-done.1 = bf16[32,32,160]{2,1,0:T(8,128)(2,1)S(1)} async-done(((bf16[32,32,160]{2,1,0:T(8,128)(2,1)}), bf16[32,32,160]{2,1,0:T(8,128)(2,1)S(1)}, u32[]{:S(2)}, u32[]{:S(2)}) %all-to-all-start.1) | async-done | bytes 327712 | tf_op jit(solution)/shard_map/all_to_all | solution.py:24
  50.1 2.3 fusion.8
  57.7 5.5 %all-to-all-start.2 = ((bf16[8,16,3584]{2,1,0:T(8,128)(2,1)}), bf16[8,16,3584]{2,1,0:T(8,128)(2,1)S(1)}, u32[]{:S(2)}, u32[]{:S(2)}) async-start(bf16[8,16,3584]{2,1,0:T(8,128)(2,1)} %broadcast_in_dim.32), calls=%async_computation.2 | async-start | bytes 1835008 | tf_op jit(solution)/shard_map/all_to_all | solution.py:24
  66.0 20.2 %all-to-all-done.2 = bf16[8,16,3584]{2,1,0:T(8,128)(2,1)S(1)} async-done(((bf16[8,16,3584]{2,1,0:T(8,128)(2,1)}), bf16[8,16,3584]{2,1,0:T(8,128)(2,1)S(1)}, u32[]{:S(2)}, u32[]{:S(2)}) %all-to-all-start.2) | async-done | bytes 917536 | tf_op jit(solution)/shard_map/all_to_all | solution.py:24
  86.1 2.0 copy-done.2
  90.8 5.9 %collective-permute-start = (bf16[128,4608]{1,0:T(8,128)(2,1)S(1)}, bf16[128,4608]{1,0:T(8,128)(2,1)S(1)}, u32[]{:S(2)}, u32[]{:S(2)}) collective-permute-start(bf16[128,4608]{1,0:T(8,128)(2,1)S(1)} %get-tuple-element.20.mine.activ.d_pre), channel_id=1, source_target_pairs={{0,32},{32,0},{1,33},{33,1},{2,34},{34,2},{3,35},{35,3},{4,36},{36... | collective-permute-start | bytes 3538952 | tf_op jit(solution)/shard_map/ppermute | solution.py:197
  96.7 4.1 %all-to-all-start.3 = ((bf16[8,16,1152]{2,1,0:T(8,128)(2,1)}), bf16[8,16,1152]{2,1,0:T(8,128)(2,1)}, u32[]{:S(2)}, u32[]{:S(2)}) async-start(bf16[8,16,1152]{2,1,0:T(8,128)(2,1)} %bitcast.117), calls=%async_computation.3 | async-start | bytes 589824 | tf_op jit(solution)/shard_map/all_to_all | solution.py:24
  101.7 2.7 %fusion.12 = f32[16,128,160]{1,2,0:T(8,128)} fusion(bf16[16,128,160]{1,2,0:T(8,128)(2,1)} %param.19, bf16[112,128]{1,0:T(8,128)(2,1)} %param.18), kind=kOutput, calls=%fused_computation.19 | convolution fusion | flops 74055680 | bytes 2650112 | tf_op jit(solution)/shard_map/lf,bld->bfd/dot_general | solution.py:204
  104.4 5.5 %shard_map.154 = bf16[4,8,224,128]{3,2,1,0:T(8,128)(2,1)S(1)} custom-call(s32[1]{0:T(128)} %bitcast.15.me, bf16[128,4608]{1,0:T(8,128)(2,1)S(1)} %get-tuple-element.20.mine.activ.d_pre, bf16[128,4608]{1,0:T(8,128)(2,1)S(1)} %collective-permute-done.other.activ_other.d_pre_other, bf16[128,4608]{1,0:T(8,128)(2,1)S(1)} %get-tuple-element.20.mine.activ.d_pre, ...), custom_call_target="tpu_custom_call" | custom-call | flops 939524096 | bytes 6000000 | tf_op jit(solution)/shard_map/pallas_call | solution.py:130
  111.2 2.7 %all-to-all-done.3 = bf16[8,16,1152]{2,1,0:T(8,128)(2,1)} async-done(((bf16[8,16,1152]{2,1,0:T(8,128)(2,1)}), bf16[8,16,1152]{2,1,0:T(8,128)(2,1)}, u32[]{:S(2)}, u32[]{:S(2)}) %all-to-all-start.3) | async-done | bytes 294944 | tf_op jit(solution)/shard_map/all_to_all | solution.py:24
  118.5 2.3 fusion.13
  121.6 2.3 fusion.18
  124.6 4.4 %collective-permute-start.1 = (bf16[64,2560]{1,0:T(8,128)(2,1)}, bf16[64,2560]{1,0:T(8,128)(2,1)}, u32[]{:S(2)}, u32[]{:S(2)}) collective-permute-start(bf16[64,2560]{1,0:T(8,128)(2,1)} %slice.102), channel_id=1, source_target_pairs={{0,4},{1,5},{2,6},{3,7},{4,0},{5,1},{6,2},{7,3},{8,12},{9,13},{10,... | collective-permute-start | bytes 983048 | tf_op jit(solution)/shard_map/ppermute | solution.py:48
  131.7 6.4 %all-to-all-start.4 = ((bf16[32,40,256]{2,1,0:T(8,128)(2,1)}), bf16[32,40,256]{2,1,0:T(8,128)(2,1)S(1)}, u32[]{:S(2)}, u32[]{:S(2)}) async-start(bf16[32,40,256]{2,1,0:T(8,128)(2,1)} %pad_maximum_fusion.1), calls=%async_computation.4 | async-start | bytes 1310720 | tf_op jit(solution)/shard_map/all_to_all | solution.py:24
  138.1 9.4 %collective-permute-done.1 = bf16[64,2560]{1,0:T(8,128)(2,1)} collective-permute-done((bf16[64,2560]{1,0:T(8,128)(2,1)}, bf16[64,2560]{1,0:T(8,128)(2,1)}, u32[]{:S(2)}, u32[]{:S(2)}) %collective-permute-start.1) | collective-permute-done | bytes 327712 | tf_op jit(solution)/shard_map/ppermute | solution.py:48
  150.5 17.7 %collective-permute-done.2 = bf16[32,2560]{1,0:T(8,128)(2,1)S(1)} collective-permute-done((bf16[32,2560]{1,0:T(8,128)(2,1)S(1)}, bf16[32,2560]{1,0:T(8,128)(2,1)S(1)}, u32[]{:S(2)}, u32[]{:S(2)}) %collective-permute-start.2) | collective-permute-done | bytes 163872 | tf_op jit(solution)/shard_map/ppermute | solution.py:48
  172.5 10.8 %all-to-all-start.5 = ((bf16[16,88,128]{2,1,0:T(8,128)(2,1)}), bf16[16,88,128]{2,1,0:T(8,128)(2,1)S(1)}, u32[]{:S(2)}, u32[]{:S(2)}) async-start(bf16[16,88,128]{2,1,0:T(8,128)(2,1)} %pad_maximum_fusion.2), calls=%async_computation.6 | async-start | bytes 720896 | tf_op jit(solution)/shard_map/all_to_all | solution.py:24
  184.1 13.0 %all-to-all-done.5 = bf16[16,88,128]{2,1,0:T(8,128)(2,1)S(1)} async-done(((bf16[16,88,128]{2,1,0:T(8,128)(2,1)}), bf16[16,88,128]{2,1,0:T(8,128)(2,1)S(1)}, u32[]{:S(2)}, u32[]{:S(2)}) %all-to-all-start.5) | async-done | bytes 360480 | tf_op jit(solution)/shard_map/all_to_all | solution.py:24
  198.0 3.4 %all-to-all-start.6 = ((bf16[16,88,128]{2,1,0:T(8,128)(2,1)}), bf16[16,88,128]{2,1,0:T(8,128)(2,1)S(1)}, u32[]{:S(2)}, u32[]{:S(2)}) async-start(bf16[16,88,128]{2,1,0:T(8,128)(2,1)} %broadcast_in_dim.36), calls=%async_computation.7 | async-start | bytes 720896 | tf_op jit(solution)/shard_map/all_to_all | solution.py:24
  203.5 2.6 %fusion.14 = bf16[16,128,160]{1,2,0:T(8,128)(2,1)} fusion(f32[16,112,160]{1,2,0:T(8,128)} %convolution_bitcast_fusion.1, f32[16,16,160]{1,2,0:T(8,128)S(1)} %copy.89, bf16[2048,160]{0,1:T(8,128)(2,1)S(1)} %copy-done.8), kind=kLoop, calls=%fused_computation.22 | loop fusion | flops 1310720 | bytes 2621440 | tf_op jit(solution)/shard_map/convert_element_type | solution.py:276
  206.1 17.2 %reduce-scatter.5.cloned.1.call-done = bf16[224,128]{1,0:T(8,128)(2,1)} async-done(((bf16[1792,128]{1,0:T(8,128)(2,1)}), bf16[224,128]{1,0:T(8,128)(2,1)}) %reduce-scatter.5.cloned.1.call-update) | async-done | bytes 57360 | tf_op jit(solution)/shard_map/reduce_scatter | solution.py:37
  (145 shorter events, 43.6 us)
Async XLA Ops:
  7.2 23.6 %copy-start = (bf16[1024,160]{0,1:T(8,128)(2,1)S(1)}, bf16[1024,160]{0,1:T(8,128)(2,1)}, u32[]{:S(2)}) copy-start(bf16[1024,160]{0,1:T(8,128)(2,1)} %param.10) | copy-start | bytes 983044
  7.2 79.0 %all-gather.2.cloned.1.call-start = ((), (), s32[]{:S(2)}) async-start(), calls=%async_computation.9 | async-start | bytes 4587520 | tf_op jit(solution)/shard_map/all_gather | solution.py:33
  31.8 5.1 %copy-start.6 = (bf16[16,128,160]{1,2,0:T(8,128)(2,1)S(1)}, bf16[16,128,160]{1,2,0:T(8,128)(2,1)}, u32[]{:S(2)}) copy-start(bf16[16,128,160]{1,2,0:T(8,128)(2,1)} %param.19) | copy-start | bytes 1966084
  31.8 5.6 %copy-start.21 = (s32[1,1,32]{2,1,0:T(1,128)S(1)}, s32[1,1,32]{2,1,0:T(1,128)}, u32[]{:S(2)}) copy-start(s32[1,1,32]{2,1,0:T(1,128)} %param.12) | copy-start | bytes 388
  32.8 17.2 %copy-start.22 = (s32[16,128]{1,0:T(8,128)S(1)}, s32[16,128]{1,0:T(8,128)}, u32[]{:S(2)}) copy-start(s32[16,128]{1,0:T(8,128)} %param.13) | copy-start | bytes 24580
  32.8 17.0 %all-to-all-start.1 = ((bf16[32,32,160]{2,1,0:T(8,128)(2,1)}), bf16[32,32,160]{2,1,0:T(8,128)(2,1)S(1)}, u32[]{:S(2)}, u32[]{:S(2)}) async-start(bf16[32,32,160]{2,1,0:T(8,128)(2,1)} %bitcast.3), calls=%async_computation.1 | async-start | bytes 1048576 | tf_op jit(solution)/shard_map/all_to_all | solution.py:24
  52.6 11.7 %copy-start.4 = (bf16[20,8,16,128]{3,2,1,0:T(8,128)(2,1)}, bf16[20,8,16,128]{3,2,1,0:T(8,128)(2,1)S(1)}, u32[]{:S(2)}) copy-start(bf16[20,8,16,128]{3,2,1,0:T(8,128)(2,1)S(1)} %copy.94) | copy-start | bytes 1966084
  57.7 28.4 %all-to-all-start.2 = ((bf16[8,16,3584]{2,1,0:T(8,128)(2,1)}), bf16[8,16,3584]{2,1,0:T(8,128)(2,1)S(1)}, u32[]{:S(2)}, u32[]{:S(2)}) async-start(bf16[8,16,3584]{2,1,0:T(8,128)(2,1)} %broadcast_in_dim.32), calls=%async_computation.2 | async-start | bytes 1835008 | tf_op jit(solution)/shard_map/all_to_all | solution.py:24
  90.8 13.6 %collective-permute-start = (bf16[128,4608]{1,0:T(8,128)(2,1)S(1)}, bf16[128,4608]{1,0:T(8,128)(2,1)S(1)}, u32[]{:S(2)}, u32[]{:S(2)}) collective-permute-start(bf16[128,4608]{1,0:T(8,128)(2,1)S(1)} %get-tuple-element.20.mine.activ.d_pre), channel_id=1, source_target_pairs={{0,32},{32,0},{1,33},{33,1},{2,34},{34,2},{3,35},{35,3},{4,36},{36... | collective-permute-start | bytes 3538952 | tf_op jit(solution)/shard_map/ppermute | solution.py:197
  96.7 17.2 %all-to-all-start.3 = ((bf16[8,16,1152]{2,1,0:T(8,128)(2,1)}), bf16[8,16,1152]{2,1,0:T(8,128)(2,1)}, u32[]{:S(2)}, u32[]{:S(2)}) async-start(bf16[8,16,1152]{2,1,0:T(8,128)(2,1)} %bitcast.117), calls=%async_computation.3 | async-start | bytes 589824 | tf_op jit(solution)/shard_map/all_to_all | solution.py:24
  100.8 69.4 %reduce-scatter.3.cloned.1.call-start = ((), (), s32[]{:S(2)}) async-start(), calls=%async_computation.10 | async-start | bytes 2293760 | tf_op jit(solution)/shard_map/reduce_scatter | solution.py:37
  111.1 3.8 %copy-start.18 = (f32[16]{0:T(128)S(1)}, f32[16]{0:T(128)}, u32[]{:S(2)}) copy-start(f32[16]{0:T(128)} %copy-done.17) | copy-start | bytes 196
  111.2 5.0 %copy-start.8 = (bf16[2048,160]{0,1:T(8,128)(2,1)S(1)}, bf16[2048,160]{0,1:T(8,128)(2,1)}, u32[]{:S(2)}) copy-start(bf16[2048,160]{0,1:T(8,128)(2,1)} %copy-done.7) | copy-start | bytes 1966084
  123.9 5.8 %copy-start.5 = (bf16[20,8,16,128]{3,2,1,0:T(8,128)(2,1)S(1)}, bf16[20,8,16,128]{3,2,1,0:T(8,128)(2,1)}, u32[]{:S(2)}) copy-start(bf16[20,8,16,128]{3,2,1,0:T(8,128)(2,1)} %copy-done.4) | copy-start | bytes 1966084
  124.6 5.8 %copy-start.16 = (bf16[1024]{0:T(1024)(128)(2,1)S(1)}, bf16[1024]{0:T(1024)(128)(2,1)}, u32[]{:S(2)}) copy-start(bf16[1024]{0:T(1024)(128)(2,1)} %get-tuple-element.52) | copy-start | bytes 6148
  124.6 22.8 %collective-permute-start.1 = (bf16[64,2560]{1,0:T(8,128)(2,1)}, bf16[64,2560]{1,0:T(8,128)(2,1)}, u32[]{:S(2)}, u32[]{:S(2)}) collective-permute-start(bf16[64,2560]{1,0:T(8,128)(2,1)} %slice.102), channel_id=1, source_target_pairs={{0,4},{1,5},{2,6},{3,7},{4,0},{5,1},{6,2},{7,3},{8,12},{9,13},{10,... | collective-permute-start | bytes 983048 | tf_op jit(solution)/shard_map/ppermute | solution.py:48
  131.7 38.4 %all-to-all-start.4 = ((bf16[32,40,256]{2,1,0:T(8,128)(2,1)}), bf16[32,40,256]{2,1,0:T(8,128)(2,1)S(1)}, u32[]{:S(2)}, u32[]{:S(2)}) async-start(bf16[32,40,256]{2,1,0:T(8,128)(2,1)} %pad_maximum_fusion.1), calls=%async_computation.4 | async-start | bytes 1310720 | tf_op jit(solution)/shard_map/all_to_all | solution.py:24
  148.5 21.9 %copy-start.20 = (s32[1024]{0:T(1024)S(1)}, s32[1024]{0:T(1024)}, u32[]{:S(2)}) copy-start(s32[1024]{0:T(1024)} %copy-done.19) | copy-start | bytes 12292
  148.6 19.6 %collective-permute-start.2 = (bf16[32,2560]{1,0:T(8,128)(2,1)S(1)}, bf16[32,2560]{1,0:T(8,128)(2,1)S(1)}, u32[]{:S(2)}, u32[]{:S(2)}) collective-permute-start(bf16[32,2560]{1,0:T(8,128)(2,1)S(1)} %slice.128), channel_id=1, source_target_pairs={{0,2},{1,3},{2,0},{3,1},{4,6},{5,7},{6,4},{7,5},{8,10},{9,11},{10,... | collective-permute-start | bytes 491528 | tf_op jit(solution)/shard_map/ppermute | solution.py:48
  168.2 15.9 %collective-permute-start.3 = (bf16[16,2560]{1,0:T(8,128)(2,1)S(1)}, bf16[16,2560]{1,0:T(8,128)(2,1)S(1)}, u32[]{:S(2)}, u32[]{:S(2)}) collective-permute-start(bf16[16,2560]{1,0:T(8,128)(2,1)S(1)} %slice.130), channel_id=1, source_target_pairs={{0,1},{1,0},{2,3},{3,2},{4,5},{5,4},{6,7},{7,6},{8,9},{9,8},{10,11... | collective-permute-start | bytes 245768 | tf_op jit(solution)/shard_map/ppermute | solution.py:48
  172.5 24.6 %all-to-all-start.5 = ((bf16[16,88,128]{2,1,0:T(8,128)(2,1)}), bf16[16,88,128]{2,1,0:T(8,128)(2,1)S(1)}, u32[]{:S(2)}, u32[]{:S(2)}) async-start(bf16[16,88,128]{2,1,0:T(8,128)(2,1)} %pad_maximum_fusion.2), calls=%async_computation.6 | async-start | bytes 720896 | tf_op jit(solution)/shard_map/all_to_all | solution.py:24
  183.4 18.1 %copy-start.11 = (bf16[112,128]{1,0:T(8,128)(2,1)S(1)}, bf16[112,128]{1,0:T(8,128)(2,1)}, u32[]{:S(2)}) copy-start(bf16[112,128]{1,0:T(8,128)(2,1)} %param.18) | copy-start | bytes 86020
  183.4 39.9 %reduce-scatter.5.cloned.1.call-start = ((), (), s32[]{:S(2)}) async-start(), calls=%async_computation.11 | async-start | bytes 516096 | tf_op jit(solution)/shard_map/reduce_scatter | solution.py:37
  198.0 25.3 %all-to-all-start.6 = ((bf16[16,88,128]{2,1,0:T(8,128)(2,1)}), bf16[16,88,128]{2,1,0:T(8,128)(2,1)S(1)}, u32[]{:S(2)}, u32[]{:S(2)}) async-start(bf16[16,88,128]{2,1,0:T(8,128)(2,1)} %broadcast_in_dim.36), calls=%async_computation.7 | async-start | bytes 720896 | tf_op jit(solution)/shard_map/all_to_all | solution.py:24
  (13 other events, 19.5 us)
Sparse Core Ops, SparseCore 0:
  10.6 60.3 all-gather.1
  111.3 36.8 reduce-scatter.2
  187.0 36.2 reduce-scatter.4

commit v5 on v4

--- a/solution.py
+++ b/solution.py
@@ -1,5 +1,3 @@
-import functools
-
 import jax
 import jax.numpy as jnp
 from jax import lax
@@ -42,14 +40,21 @@
     return jnp.concatenate([high, value - high], axis=-1).astype(jnp.bfloat16)
 
 
-def halved(blocks, axis, step):
-    half = blocks.shape[0] // 2
-    pairs = [(i, i ^ step) for i in range(lax.axis_size(axis))]
-    other = lax.ppermute(blocks[half:], axis, pairs)
-    return (blocks[:half].astype(jnp.float32) + other.astype(jnp.float32)).astype(jnp.bfloat16)
-
-
-def network_kernel(batch, me, ring, weights, lcb, back, mlp, mine, shuffled):
+def halved(blocks, axis):
+    count, place = lax.axis_size(axis), lax.axis_index(axis)
+    step = count // 2
+    while step:
+        blocks = blocks.reshape(2, -1, blocks.shape[-1])
+        side = place // step % 2
+        keep = lax.dynamic_index_in_dim(blocks, side, keepdims=False)
+        send = lax.dynamic_index_in_dim(blocks, 1 - side, keepdims=False)
+        other = lax.ppermute(send, axis, [(i, i ^ step) for i in range(count)])
+        blocks = (keep.astype(jnp.float32) + other.astype(jnp.float32)).astype(jnp.bfloat16)
+        step //= 2
+    return blocks
+
+
+def network_kernel(ring, weights, lcb, back, mine):
     f32, bf16 = jnp.float32, jnp.bfloat16
     samples, columns = ring.shape
     split, taps = F * K, weights.shape[0]
@@ -67,37 +72,29 @@
     mine[:, columns : columns + taps] = activ
     mine[:, columns + taps :] = d_pre
     back[:, :split] = jnp.dot(d_pre, weights[:, :split], preferred_element_type=f32).astype(bf16)
-    back[:, split:] = lcb[...]
-    for block in range(samples // batch):
-        start = pl.multiple_of((me[0] ^ block) * batch, batch)
-        shuffled[pl.ds(start, batch), :] = activ[block * batch : (block + 1) * batch]
-    for start in range(0, columns - split, 512):
-        mlp[:, start : start + 512] = jnp.dot(
-            shuffled[...],
-            weights[:, split + start : split + start + 512],
-            preferred_element_type=f32,
+    for start in range(split, columns, 512):
+        back[:, start : start + 512] = jnp.dot(
+            activ, weights[:, start : start + 512], preferred_element_type=f32
         ).astype(bf16)
-
-
-def network(ring, weights, lcb, batch):
+    back[:, columns:] = lcb[...]
+
+
+def network(ring, weights, lcb):
     samples, columns = ring.shape
     taps = weights.shape[0]
-    vmem = pl.BlockSpec(memory_space=pltpu.VMEM)
     shape = lambda width: jax.ShapeDtypeStruct((samples, width), jnp.bfloat16)
     return pl.pallas_call(
-        functools.partial(network_kernel, batch),
-        in_specs=[pl.BlockSpec(memory_space=pltpu.SMEM), vmem, vmem, vmem],
-        out_shape=(shape(F * K + lcb.shape[1]), shape(columns - F * K), shape(columns + 2 * taps)),
-        scratch_shapes=[pltpu.VMEM((samples, taps), jnp.bfloat16)],
+        network_kernel,
+        out_shape=(shape(columns + lcb.shape[1]), shape(columns + 2 * taps)),
         compiler_params=pltpu.CompilerParams(vmem_limit_bytes=32 * 2**20),
         cost_estimate=pl.CostEstimate(
             flops=4 * samples * taps * columns, bytes_accessed=7_000_000, transcendentals=65536
         ),
-    )(lax.axis_index("y").reshape(1), ring, weights, lcb)
+    )(ring, weights, lcb)
 
 
 def weight_kernel(me, mine, other, activ, activ_other, d_pre, d_pre_other, out):
-    _, depth, _, _ = out.shape
+    depth = out.shape[0]
     f32 = jnp.float32
     along = (((0,), (0,)), ((), ()))
     first = me[0] == 0
@@ -115,7 +112,7 @@
                 other[:, at], right_other[...], along, preferred_element_type=f32
             )
             part = jnp.where(first, part[:rows], part[rows:])
-            out[0, z, start : start + rows] = part.astype(jnp.bfloat16)
+            out[z, 0, start : start + rows] = part.astype(jnp.bfloat16)
         start += rows
 
 
@@ -133,8 +130,8 @@
         in_specs=[
             pl.BlockSpec(memory_space=pltpu.SMEM), ring, ring, activ, activ, d_pre, d_pre
         ],
-        out_specs=pl.BlockSpec((1, depth, rows, hidden), lambda j: (j, 0, 0, 0)),
-        out_shape=jax.ShapeDtypeStruct((far, depth, rows, hidden), jnp.bfloat16),
+        out_specs=pl.BlockSpec((depth, 1, rows, hidden), lambda j: (0, j, 0, 0)),
+        out_shape=jax.ShapeDtypeStruct((depth, far, rows, hidden), jnp.bfloat16),
         compiler_params=pltpu.CompilerParams(vmem_limit_bytes=32 * 2**20),
         cost_estimate=pl.CostEstimate(
             flops=8 * samples * rows * depth * far * hidden,
@@ -192,15 +189,16 @@
     lcb_part = lcb_part.astype(bf16).reshape(near * batch, -1)
     spare = -lcb_part.shape[1] % LANES
     lcb_padded = jnp.pad(lcb_part, ((0, 0), (0, spare)))
-    back, mlp_part, mine = network(ring, weights, lcb_padded, batch)
+    back, mine = network(ring, weights, lcb_padded)
     back = exchange(back.reshape(near, batch, -1), "y")
     other = lax.ppermute(mine, "core", [(0, 1), (1, 0)])
     weight_sum = weight_products(mine, other, hidden, far, depth).reshape(-1, hidden)
     back, _ = lax.optimization_barrier((back, weight_sum))
-    weight_sum = scatter(weight_sum, "x")
+    weight_sum = scatter(weight_sum, "z")
     back = jnp.sum(back.astype(f32), axis=0)
-    d_normed = back[:, : F * K]
-    lcb_mine = back[:, F * K : F * K + lcb_part.shape[1]].astype(bf16)
+    split, end = F * K, F * K + NF * width
+    d_normed, mlp_out = back[:, :split], back[:, split:end]
+    lcb_mine = back[:, end : end + lcb_part.shape[1]].astype(bf16)
     d_linear = jnp.einsum("lf,bld->bfd", w_lcb, grad_linear, preferred_element_type=f32)
 
     gain_part = jnp.sum(d_normed * normal_part, axis=0)
@@ -222,13 +220,6 @@
     slot_grad = jnp.dot(slot_rows_hot, d_embeds, preferred_element_type=f32)
     slot_grad = slot_grad.reshape(members, CAP, width)
     slot_grad = jnp.where(live_mask[:, :, None], slot_grad, 0.0).astype(bf16)
-    slot_grad, mlp_part = lax.optimization_barrier((slot_grad, mlp_part))
-    mlp_part = halved(mlp_part, "y", near // 2)
-    step = near // 4
-    while step:
-        mlp_part = halved(mlp_part, "y", step)
-        step //= 2
-    mlp_out = mlp_part.astype(f32)
     proj_part = jnp.einsum("bfd,bdk->fk", embeds, halves(d_compressed), preferred_element_type=f32)
     proj_part = proj_part[:, :K] + proj_part[:, K:]
     small = jnp.concatenate([gain_part, proj_part.reshape(-1)]).astype(bf16).reshape(CAP, -1)
@@ -239,8 +230,6 @@
     sent = jnp.concatenate([slot_grad, jnp.broadcast_to(small[None], (members, *small.shape))], axis=2)
     lcb_sent = jnp.broadcast_to(lcb_mine[None], (members, *lcb_mine.shape))
     received = exchange(jnp.concatenate([sent, lcb_sent], axis=1), shard)
-    received, weight_sum = lax.optimization_barrier((received, weight_sum))
-    weight_sum = scatter(weight_sum, "z")
     returned = received[:, :CAP, :width].reshape(slots, width)
     small_end = width + 2 * F * K // CAP
     small = jnp.sum(received[:, :CAP, width:small_end].astype(f32), axis=0).astype(bf16)
@@ -257,11 +246,13 @@
     table_part = table_part.reshape(width, columns, LANES).transpose(1, 0, 2)
     table_part = table_part.reshape(groups, -1, LANES)
     held = table_part.shape[1]
-    total = exchange(jnp.concatenate([table_part, small], axis=1), dp)
+    total = jnp.concatenate([table_part, small], axis=1)
+    total, weight_sum = lax.optimization_barrier((total, weight_sum))
+    weight_sum = halved(weight_sum, "x")
+    total = exchange(total, dp)
     total = jnp.sum(total.astype(f32), axis=0).astype(bf16)
-    total, mlp_out = lax.optimization_barrier((total, mlp_out))
+    total, weight_sum = lax.optimization_barrier((total, weight_sum))
     total = spread(total, dp)
-    total, weight_sum = lax.optimization_barrier((total, weight_sum))
     down_count = NF * width // groups
     grad_w_down = weight_sum[:down_count].T
     grad_w_up = weight_sum[down_count:]

time: 241 us -> 221 us (0.917); the launches traced: 236 us -> 220 us
  waiting for transfers between devices: 93.3 us -> 73.1 us
  starting transfers between devices: 48.7 us -> 51.5 us
    ppermute x3 -> x2, waiting for transfers between devices: 27 us -> 2.9 us  [halved(): other = lax.ppermute(send, axis, [(i, i ^ step) for i in range(count)])]
    all_to_all x6, waiting for transfers between devices: 48.3 us -> 70.2 us  [exchange(): return lax.all_to_all(blocks, axis, split_axis=0, concat_axis=0, tiled=True)]
    reduce_scatter x2 -> x1, waiting for transfers between devices: 17.2 us -> 0.01 us  [scatter(): return lax.psum_scatter(blocks, axis, scatter_dimension=0, tiled=True)]
    all_to_all x6, starting transfers between devices: 34.2 us -> 38.7 us  [exchange(): return lax.all_to_all(blocks, axis, split_axis=0, concat_axis=0, tiled=True)]
    ppermute x3 -> x2, starting transfers between devices: 8.24 us -> 6.62 us  [halved(): other = lax.ppermute(send, axis, [(i, i ^ step) for i in range(count)])]
    unnamed x52 -> x46, local copies, waits for them, and re-layouts: 7.7 us -> 6.85 us
  transfers between devices with their start and end apart: 13 -> 11, of which waited for: 7 -> 7; matrix products, arithmetic and copies ran while one was open for 17% -> 19% of each run, Pallas kernels for 2% -> 3%
where the time goes in v5:
time: 221 us; the launch traced here: 220 us
  waiting for transfers between devices  73.1 us (33%)
  starting transfers between devices  51.5 us (23%)
  matrix products  21 us (10%)
  blocking collectives  18.9 us (9%)
  local copies, waits for them, and re-layouts  18.3 us (8%)
  between operations  14.7 us (7%)
  other arithmetic  13.6 us (6%)
  Pallas kernels  8.37 us (4%)
    all_to_all x6, waiting for transfers between devices, exchange(): return lax.all_to_all(blocks, axis, split_axis=0, concat_axis=0, tiled=True)  70.2 us
    all_to_all x6, starting transfers between devices, exchange(): return lax.all_to_all(blocks, axis, split_axis=0, concat_axis=0, tiled=True)  38.7 us
    all_to_all x1, blocking collectives, exchange(): return lax.all_to_all(blocks, axis, split_axis=0, concat_axis=0, tiled=True)  18.9 us
    unnamed x46, local copies, waits for them, and re-layouts  6.85 us
    ppermute x2, starting transfers between devices, halved(): other = lax.ppermute(send, axis, [(i, i ^ step) for i in range(count)])  6.62 us
    ppermute x1, starting transfers between devices, body(): other = lax.ppermute(mine, 'core', [(0, 1), (1, 0)])  6.08 us
    pallas_call x1, Pallas kernels, weight_products(): pl.pallas_call(weight_kernel, grid=(far,), in_specs=[pl.BlockSpec(memory_...  5.52 us
  transfers between devices with their start and end apart: 11, of which 7 were waited for; matrix products, arithmetic and copies ran while one was open for 19% of the time, Pallas kernels for 3%

profile of v5, /device:TPU:1, one launch (start us, length us, event | category | flops | bytes accessed | tf_op | source)
XLA Modules:
  0.0 219.5 jit_solution(10089032246924145792)
XLA Ops:
  10.5 18.9 %all_to_all.39 = s32[32,1,32]{2,1,0:T(1,128)S(1)} all-to-all(s32[32,1,32]{2,1,0:T(1,128)S(1)} %bitcast.150), channel_id=1, replica_groups=mesh['z'=8,'core'=2,'x'=4,'y'=8] {'x','y'}, dimensions={0} | all-to-all | bytes 8192 | tf_op jit(solution)/shard_map/all_to_all | solution.py:22
  32.8 4.0 %all-to-all-start.1 = ((bf16[32,32,160]{2,1,0:T(8,128)(2,1)}), bf16[32,32,160]{2,1,0:T(8,128)(2,1)S(1)}, u32[]{:S(2)}, u32[]{:S(2)}) async-start(bf16[32,32,160]{2,1,0:T(8,128)(2,1)} %bitcast.3), calls=%async_computation.1 | async-start | bytes 1048576 | tf_op jit(solution)/shard_map/all_to_all | solution.py:22
  37.5 12.4 %all-to-all-done.1 = bf16[32,32,160]{2,1,0:T(8,128)(2,1)S(1)} async-done(((bf16[32,32,160]{2,1,0:T(8,128)(2,1)}), bf16[32,32,160]{2,1,0:T(8,128)(2,1)S(1)}, u32[]{:S(2)}, u32[]{:S(2)}) %all-to-all-start.1) | async-done | bytes 327712 | tf_op jit(solution)/shard_map/all_to_all | solution.py:22
  50.1 2.3 %fusion.8 = bf16[2048,160]{0,1:T(8,128)(2,1)S(1)} fusion(bf16[1024,160]{1,0:T(8,128)(2,1)S(1)} %bitcast.144, s32[2048]{0:T(1024)S(1)} %bitcast.152), kind=kOutput, calls=%fused_computation.11 | convolution fusion | flops 673513472 | bytes 991232 | tf_op jit(solution)/shard_map/dot_general | solution.py:174
  57.7 5.5 %all-to-all-start.2 = ((bf16[8,16,3584]{2,1,0:T(8,128)(2,1)}), bf16[8,16,3584]{2,1,0:T(8,128)(2,1)S(1)}, u32[]{:S(2)}, u32[]{:S(2)}) async-start(bf16[8,16,3584]{2,1,0:T(8,128)(2,1)} %broadcast_in_dim.32), calls=%async_computation.2 | async-start | bytes 1835008 | tf_op jit(solution)/shard_map/all_to_all | solution.py:22
  64.1 22.1 %all-to-all-done.2 = bf16[8,16,3584]{2,1,0:T(8,128)(2,1)S(1)} async-done(((bf16[8,16,3584]{2,1,0:T(8,128)(2,1)}), bf16[8,16,3584]{2,1,0:T(8,128)(2,1)S(1)}, u32[]{:S(2)}, u32[]{:S(2)}) %all-to-all-start.2) | async-done | bytes 917536 | tf_op jit(solution)/shard_map/all_to_all | solution.py:22
  88.2 2.9 %shard_map.153 = (bf16[128,3712]{1,0:T(8,128)(2,1)}, bf16[128,4608]{1,0:T(8,128)(2,1)S(1)}) custom-call(bf16[128,3584]{1,0:T(8,128)(2,1)S(1)} %bitcast.131, bf16[512,3584]{1,0:T(8,128)(2,1)S(1)} %copy-done.2, bf16[128,128]{1,0:T(8,128)(2,1)S(1)} %pad.12.lcb), custom_call_target="tpu_custom_call" | custom-call | flops 939524096 | bytes 7000000 | tf_op jit(solution)/shard_map/pallas_call | solution.py:86
  91.0 4.2 %all-to-all-start.3 = ((bf16[8,16,3712]{2,1,0:T(8,128)(2,1)}), bf16[8,16,3712]{2,1,0:T(8,128)(2,1)}, u32[]{:S(2)}, u32[]{:S(2)}) async-start(bf16[8,16,3712]{2,1,0:T(8,128)(2,1)} %bitcast.11), calls=%async_computation.3 | async-start | bytes 1900544 | tf_op jit(solution)/shard_map/all_to_all | solution.py:22
  95.3 6.1 %collective-permute-start = (bf16[128,4608]{1,0:T(8,128)(2,1)S(1)}, bf16[128,4608]{1,0:T(8,128)(2,1)S(1)}, u32[]{:S(2)}, u32[]{:S(2)}) collective-permute-start(bf16[128,4608]{1,0:T(8,128)(2,1)S(1)} %get-tuple-element.15.mine.activ.d_pre), channel_id=1, source_target_pairs={{0,32},{32,0},{1,33},{33,1},{2,34},{34,2},{3,35},{35,3},{4,36},{36... | collective-permute-start | bytes 3538952 | tf_op jit(solution)/shard_map/ppermute | solution.py:194
  102.0 2.8 %fusion.12 = f32[16,128,160]{1,2,0:T(8,128)} fusion(bf16[16,128,160]{1,2,0:T(8,128)(2,1)} %param.19, bf16[112,128]{1,0:T(8,128)(2,1)} %param.18), kind=kOutput, calls=%fused_computation.19 | convolution fusion | flops 74055680 | bytes 2650112 | tf_op jit(solution)/shard_map/lf,bld->bfd/dot_general | solution.py:202
  104.9 5.5 %shard_map.154 = bf16[8,4,224,128]{3,2,1,0:T(8,128)(2,1)S(1)} custom-call(s32[1]{0:T(128)} %bitcast.12.me, bf16[128,4608]{1,0:T(8,128)(2,1)S(1)} %get-tuple-element.15.mine.activ.d_pre, bf16[128,4608]{1,0:T(8,128)(2,1)S(1)} %collective-permute-done.other.activ_other.d_pre_other, bf16[128,4608]{1,0:T(8,128)(2,1)S(1)} %get-tuple-element.15.mine.activ.d_pre, ...), custom_call_target="tpu_custom_call" | custom-call | flops 939524096 | bytes 6000000 | tf_op jit(solution)/shard_map/pallas_call | solution.py:127
  111.7 7.1 %all-to-all-done.3 = bf16[8,16,3712]{2,1,0:T(8,128)(2,1)} async-done(((bf16[8,16,3712]{2,1,0:T(8,128)(2,1)}), bf16[8,16,3712]{2,1,0:T(8,128)(2,1)}, u32[]{:S(2)}, u32[]{:S(2)}) %all-to-all-start.3) | async-done | bytes 950304 | tf_op jit(solution)/shard_map/all_to_all | solution.py:22
  127.2 2.1 convolution_bitcast_fusion
  129.4 2.3 %fusion.13 = bf16[16,128,160]{1,2,0:T(8,128)(2,1)S(1)} fusion(f32[16,128,160]{1,2,0:T(8,128)S(1)} %convolution_bitcast_fusion, f32[16,128,160]{1,2,0:T(8,128)S(1)} %copy-done.6, f32[16,128,8]{1,2,0:T(8,128)S(1)} %copy.85, f32[16,160,8]{1,2,0:T(8,128)S(1)} %copy.75), kind=kOutput, calls=%fused_computation.21 | convolution fusion | flops 32440320 | bytes 3424256 | tf_op jit(solution)/shard_map/bfk,bdk->bfd/dot_general | solution.py:214
  135.1 5.4 %all-to-all-start.4 = ((bf16[32,40,256]{2,1,0:T(8,128)(2,1)}), bf16[32,40,256]{2,1,0:T(8,128)(2,1)S(1)}, u32[]{:S(2)}, u32[]{:S(2)}) async-start(bf16[32,40,256]{2,1,0:T(8,128)(2,1)} %pad_maximum_fusion.1), calls=%async_computation.4 | async-start | bytes 1310720 | tf_op jit(solution)/shard_map/all_to_all | solution.py:22
  140.5 13.6 %all-to-all-done.4 = bf16[32,40,256]{2,1,0:T(8,128)(2,1)S(1)} async-done(((bf16[32,40,256]{2,1,0:T(8,128)(2,1)}), bf16[32,40,256]{2,1,0:T(8,128)(2,1)S(1)}, u32[]{:S(2)}, u32[]{:S(2)}) %all-to-all-start.4) | async-done | bytes 655392 | tf_op jit(solution)/shard_map/all_to_all | solution.py:22
  157.5 4.2 %collective-permute-start.1 = (bf16[448,128]{1,0:T(8,128)(2,1)S(1)}, bf16[448,128]{1,0:T(8,128)(2,1)S(1)}, u32[]{:S(2)}, u32[]{:S(2)}) collective-permute-start(bf16[448,128]{1,0:T(8,128)(2,1)S(1)} %dynamic-slice_bitcast_fusion), channel_id=1, source_target_pairs={{0,16},{8,24},{16,0},{24,8},{1,17},{9,25},{17,1},{25,9},{2,18},{10... | collective-permute-start | bytes 344072 | tf_op jit(solution)/shard_map/ppermute | solution.py:51
  161.7 16.2 %all-to-all-start.5 = ((bf16[16,88,128]{2,1,0:T(8,128)(2,1)}), bf16[16,88,128]{2,1,0:T(8,128)(2,1)S(1)}, u32[]{:S(2)}, u32[]{:S(2)}) async-start(bf16[16,88,128]{2,1,0:T(8,128)(2,1)} %pad_maximum_fusion.2), calls=%async_computation.6 | async-start | bytes 720896 | tf_op jit(solution)/shard_map/all_to_all | solution.py:22
  178.8 2.4 %collective-permute-start.2 = (bf16[224,128]{1,0:T(8,128)(2,1)S(1)}, bf16[224,128]{1,0:T(8,128)(2,1)S(1)}, u32[]{:S(2)}, u32[]{:S(2)}) collective-permute-start(bf16[224,128]{1,0:T(8,128)(2,1)S(1)} %dynamic-slice_bitcast_fusion.1), channel_id=1, source_target_pairs={{0,8},{8,0},{16,24},{24,16},{1,9},{9,1},{17,25},{25,17},{2,10},{10... | collective-permute-start | bytes 172040 | tf_op jit(solution)/shard_map/ppermute | solution.py:51
  181.2 2.9 %collective-permute-done.2 = bf16[224,128]{1,0:T(8,128)(2,1)S(1)} collective-permute-done((bf16[224,128]{1,0:T(8,128)(2,1)S(1)}, bf16[224,128]{1,0:T(8,128)(2,1)S(1)}, u32[]{:S(2)}, u32[]{:S(2)}) %collective-permute-start.2) | collective-permute-done | bytes 57376 | tf_op jit(solution)/shard_map/ppermute | solution.py:51
  184.1 7.6 %all-to-all-done.5 = bf16[16,88,128]{2,1,0:T(8,128)(2,1)S(1)} async-done(((bf16[16,88,128]{2,1,0:T(8,128)(2,1)}), bf16[16,88,128]{2,1,0:T(8,128)(2,1)S(1)}, u32[]{:S(2)}, u32[]{:S(2)}) %all-to-all-start.5) | async-done | bytes 360480 | tf_op jit(solution)/shard_map/all_to_all | solution.py:22
  192.5 3.4 %all-to-all-start.6 = ((bf16[16,88,128]{2,1,0:T(8,128)(2,1)}), bf16[16,88,128]{2,1,0:T(8,128)(2,1)S(1)}, u32[]{:S(2)}, u32[]{:S(2)}) async-start(bf16[16,88,128]{2,1,0:T(8,128)(2,1)} %broadcast_in_dim.36), calls=%async_computation.7 | async-start | bytes 720896 | tf_op jit(solution)/shard_map/all_to_all | solution.py:22
  198.0 2.6 %fusion.14 = bf16[16,128,160]{1,2,0:T(8,128)(2,1)} fusion(f32[16,112,160]{1,2,0:T(8,128)} %convolution_bitcast_fusion.2, f32[16,16,160]{1,2,0:T(8,128)S(1)} %copy.82, bf16[2048,160]{0,1:T(8,128)(2,1)S(1)} %copy-done.5), kind=kLoop, calls=%fused_computation.23 | loop fusion | flops 1310720 | bytes 2621440 | tf_op jit(solution)/shard_map/convert_element_type | solution.py:267
  201.8 7.5 %all-to-all-done.6 = bf16[16,88,128]{2,1,0:T(8,128)(2,1)S(1)} async-done(((bf16[16,88,128]{2,1,0:T(8,128)(2,1)}), bf16[16,88,128]{2,1,0:T(8,128)(2,1)S(1)}, u32[]{:S(2)}, u32[]{:S(2)}) %all-to-all-start.6) | async-done | bytes 360480 | tf_op jit(solution)/shard_map/all_to_all | solution.py:22
  (133 shorter events, 40.8 us)
Async XLA Ops:
  7.2 23.6 %copy-start = (bf16[1024,160]{0,1:T(8,128)(2,1)S(1)}, bf16[1024,160]{0,1:T(8,128)(2,1)}, u32[]{:S(2)}) copy-start(bf16[1024,160]{0,1:T(8,128)(2,1)} %param.10) | copy-start | bytes 983044
  7.2 79.0 %all-gather.2.cloned.1.call-start = ((), (), s32[]{:S(2)}) async-start(), calls=%async_computation.8 | async-start | bytes 4587520 | tf_op jit(solution)/shard_map/all_gather | solution.py:31
  8.4 2.1 copy-start.9
  31.8 5.1 %copy-start.3 = (bf16[16,128,160]{1,2,0:T(8,128)(2,1)S(1)}, bf16[16,128,160]{1,2,0:T(8,128)(2,1)}, u32[]{:S(2)}) copy-start(bf16[16,128,160]{1,2,0:T(8,128)(2,1)} %param.19) | copy-start | bytes 1966084
  31.8 5.6 %copy-start.18 = (s32[1,1,32]{2,1,0:T(1,128)S(1)}, s32[1,1,32]{2,1,0:T(1,128)}, u32[]{:S(2)}) copy-start(s32[1,1,32]{2,1,0:T(1,128)} %param.12) | copy-start | bytes 388
  32.8 17.2 %copy-start.19 = (s32[16,128]{1,0:T(8,128)S(1)}, s32[16,128]{1,0:T(8,128)}, u32[]{:S(2)}) copy-start(s32[16,128]{1,0:T(8,128)} %param.13) | copy-start | bytes 24580
  32.8 17.0 %all-to-all-start.1 = ((bf16[32,32,160]{2,1,0:T(8,128)(2,1)}), bf16[32,32,160]{2,1,0:T(8,128)(2,1)S(1)}, u32[]{:S(2)}, u32[]{:S(2)}) async-start(bf16[32,32,160]{2,1,0:T(8,128)(2,1)} %bitcast.3), calls=%async_computation.1 | async-start | bytes 1048576 | tf_op jit(solution)/shard_map/all_to_all | solution.py:22
  52.4 2.7 %copy-start.4 = (bf16[2048,160]{0,1:T(8,128)(2,1)}, bf16[2048,160]{0,1:T(8,128)(2,1)S(1)}, u32[]{:S(2)}) copy-start(bf16[2048,160]{0,1:T(8,128)(2,1)S(1)} %fusion.8) | copy-start | bytes 1966084
  56.3 63.9 %copy-start.12 = (f32[16]{0:T(128)}, f32[16]{0:T(128)S(1)}, u32[]{:S(2)}) copy-start(f32[16]{0:T(128)S(1)} %broadcast_multiply_fusion.2) | copy-start | bytes 196
  57.7 28.4 %all-to-all-start.2 = ((bf16[8,16,3584]{2,1,0:T(8,128)(2,1)}), bf16[8,16,3584]{2,1,0:T(8,128)(2,1)S(1)}, u32[]{:S(2)}, u32[]{:S(2)}) async-start(bf16[8,16,3584]{2,1,0:T(8,128)(2,1)} %broadcast_in_dim.32), calls=%async_computation.2 | async-start | bytes 1835008 | tf_op jit(solution)/shard_map/all_to_all | solution.py:22
  91.0 27.8 %all-to-all-start.3 = ((bf16[8,16,3712]{2,1,0:T(8,128)(2,1)}), bf16[8,16,3712]{2,1,0:T(8,128)(2,1)}, u32[]{:S(2)}, u32[]{:S(2)}) async-start(bf16[8,16,3712]{2,1,0:T(8,128)(2,1)} %bitcast.11), calls=%async_computation.3 | async-start | bytes 1900544 | tf_op jit(solution)/shard_map/all_to_all | solution.py:22
  95.3 61.2 %reduce-scatter.2.cloned.1.call-start = ((), (), s32[]{:S(2)}) async-start(), calls=%async_computation.9 | async-start | bytes 2064384 | tf_op jit(solution)/shard_map/reduce_scatter | solution.py:35
  95.3 9.6 %collective-permute-start = (bf16[128,4608]{1,0:T(8,128)(2,1)S(1)}, bf16[128,4608]{1,0:T(8,128)(2,1)S(1)}, u32[]{:S(2)}, u32[]{:S(2)}) collective-permute-start(bf16[128,4608]{1,0:T(8,128)(2,1)S(1)} %get-tuple-element.15.mine.activ.d_pre), channel_id=1, source_target_pairs={{0,32},{32,0},{1,33},{33,1},{2,34},{34,2},{3,35},{35,3},{4,36},{36... | collective-permute-start | bytes 3538952 | tf_op jit(solution)/shard_map/ppermute | solution.py:194
  111.7 8.5 %copy-start.15 = (f32[16]{0:T(128)S(1)}, f32[16]{0:T(128)}, u32[]{:S(2)}) copy-start(f32[16]{0:T(128)} %copy-done.14) | copy-start | bytes 196
  111.7 10.3 %copy-start.5 = (bf16[2048,160]{0,1:T(8,128)(2,1)S(1)}, bf16[2048,160]{0,1:T(8,128)(2,1)}, u32[]{:S(2)}) copy-start(bf16[2048,160]{0,1:T(8,128)(2,1)} %copy-done.4) | copy-start | bytes 1966084
  123.8 3.3 %copy-start.13 = (bf16[1024]{0:T(1024)(128)(2,1)S(1)}, bf16[1024]{0:T(1024)(128)(2,1)}, u32[]{:S(2)}) copy-start(bf16[1024]{0:T(1024)(128)(2,1)} %get-tuple-element.42) | copy-start | bytes 6148
  125.2 4.1 %copy-start.6 = (f32[16,128,160]{1,2,0:T(8,128)S(1)}, f32[16,128,160]{1,2,0:T(8,128)}, u32[]{:S(2)}) copy-start(f32[16,128,160]{1,2,0:T(8,128)} %fusion.12) | copy-start | bytes 3932164
  135.1 19.1 %copy-start.17 = (s32[1024]{0:T(1024)S(1)}, s32[1024]{0:T(1024)}, u32[]{:S(2)}) copy-start(s32[1024]{0:T(1024)} %copy-done.16) | copy-start | bytes 12292
  135.1 19.1 %all-to-all-start.4 = ((bf16[32,40,256]{2,1,0:T(8,128)(2,1)}), bf16[32,40,256]{2,1,0:T(8,128)(2,1)S(1)}, u32[]{:S(2)}, u32[]{:S(2)}) async-start(bf16[32,40,256]{2,1,0:T(8,128)(2,1)} %pad_maximum_fusion.1), calls=%async_computation.4 | async-start | bytes 1310720 | tf_op jit(solution)/shard_map/all_to_all | solution.py:22
  157.4 38.5 %copy-start.7 = (bf16[112,128]{1,0:T(8,128)(2,1)S(1)}, bf16[112,128]{1,0:T(8,128)(2,1)}, u32[]{:S(2)}) copy-start(bf16[112,128]{1,0:T(8,128)(2,1)} %param.18) | copy-start | bytes 86020
  157.5 20.4 %collective-permute-start.1 = (bf16[448,128]{1,0:T(8,128)(2,1)S(1)}, bf16[448,128]{1,0:T(8,128)(2,1)S(1)}, u32[]{:S(2)}, u32[]{:S(2)}) collective-permute-start(bf16[448,128]{1,0:T(8,128)(2,1)S(1)} %dynamic-slice_bitcast_fusion), channel_id=1, source_target_pairs={{0,16},{8,24},{16,0},{24,8},{1,17},{9,25},{17,1},{25,9},{2,18},{10... | collective-permute-start | bytes 344072 | tf_op jit(solution)/shard_map/ppermute | solution.py:51
  161.7 30.0 %all-to-all-start.5 = ((bf16[16,88,128]{2,1,0:T(8,128)(2,1)}), bf16[16,88,128]{2,1,0:T(8,128)(2,1)S(1)}, u32[]{:S(2)}, u32[]{:S(2)}) async-start(bf16[16,88,128]{2,1,0:T(8,128)(2,1)} %pad_maximum_fusion.2), calls=%async_computation.6 | async-start | bytes 720896 | tf_op jit(solution)/shard_map/all_to_all | solution.py:22
  178.8 5.3 %collective-permute-start.2 = (bf16[224,128]{1,0:T(8,128)(2,1)S(1)}, bf16[224,128]{1,0:T(8,128)(2,1)S(1)}, u32[]{:S(2)}, u32[]{:S(2)}) collective-permute-start(bf16[224,128]{1,0:T(8,128)(2,1)S(1)} %dynamic-slice_bitcast_fusion.1), channel_id=1, source_target_pairs={{0,8},{8,0},{16,24},{24,16},{1,9},{9,1},{17,25},{25,17},{2,10},{10... | collective-permute-start | bytes 172040 | tf_op jit(solution)/shard_map/ppermute | solution.py:51
  192.5 16.8 %all-to-all-start.6 = ((bf16[16,88,128]{2,1,0:T(8,128)(2,1)}), bf16[16,88,128]{2,1,0:T(8,128)(2,1)S(1)}, u32[]{:S(2)}, u32[]{:S(2)}) async-start(bf16[16,88,128]{2,1,0:T(8,128)(2,1)} %broadcast_in_dim.36), calls=%async_computation.7 | async-start | bytes 720896 | tf_op jit(solution)/shard_map/all_to_all | solution.py:22
  (8 other events, 10.6 us)
Sparse Core Ops, SparseCore 0:
  10.6 60.3 all-gather.1
  111.8 44.0 reduce-scatter.1
